TPU v7x, 512 devices: a whole 4x4x16 slice. The times are simulated.
512 devices in a mesh: flow: 64 (over x, z), trans: 8 (over y, core).
Axes of the slice: x: 4, y: 4, z: 16, core: 2. Of those that a mesh axis runs over, the one named last changes fastest.
Arguments:
- basis_flux: bfloat16 [64, 1024, 1024], P('flow', 'trans'), may hold values from -0.125 to 0.125
- owner_cell: int32 [64, 1024], P('flow', 'trans'), may hold values from 0 to 1023
- clogged: int32 [64, 1024], P('flow', 'trans'), may hold values 0 or 1
- conductance: float32 [64, 1024], P('flow', 'trans'), may hold values from 0.1 to 1
- live_count: int32 [64, 8], P('flow', 'trans'), may hold values from 32 to 128
- coupling: float32 [64, 1024], P('flow'), may hold values from 1.8 to 2
- leakage: float32 [64, 1024], P('flow'), may hold values from 0.02 to 0.08
- source: float32 [64, 1024], P('flow'), may hold values from -6 to 6
Outputs:
- pressure: float32 [64, 1024], P('flow', 'trans')
All inputs are finite; a program needn't handle non-finite values. No bound on the sum of `clogged` on one device may be relied on, other than what follows from the above.
Results may differ from a plain program's by a relative error of at most 0.0003.
The roundings to bfloat16 on the way count: a program that leaves them out, or rounds other values in their place, can miss the bound.
Values may be sent and summed in bfloat16 or wider, within the bound.
A program may use at most 64 MiB of HBM per device.

v0:
```python
import math

import jax
import jax.numpy as jnp
from jax import lax
from jax.sharding import PartitionSpec as P


def from_behind(value, axis, steps):
    count = lax.axis_size(axis)
    initial, last = (max(0, -steps), min(count, count - steps))
    return lax.ppermute(value, axis, [(source, source + steps) for source in range(initial, last)])


def add_block(running, flux_rows, owner_rows, weight_rows):
    columns = lax.iota(jnp.int32, running.shape[1])
    picked = jnp.where(
        owner_rows[:, None] == columns[None, :], weight_rows[:, None], jnp.zeros((), jnp.bfloat16)
    )
    return running + lax.dot_general(
        picked, flux_rows, (((0,), (0,)), ((), ())), preferred_element_type=jnp.float32
    )


def accumulate(flux_rows, owners, weights, live_rows, empty):
    step_rows = math.gcd(flux_rows.shape[0], 512)

    def block_step(block_index, running):
        start = block_index * step_rows
        return add_block(running, flux_rows, owners, weights)

    return lax.fori_loop(0, (live_rows + step_rows - 1) // step_rows, block_step, empty)


def matvec(matrix, vector):
    return jnp.dot(
        matrix, vector, precision=lax.Precision.HIGHEST, preferred_element_type=jnp.float32
    )


def per_device(basis_flux, owner_cell, clogged, conductance, live_count, coupling, leakage, source):
    flux_rows = basis_flux[0]
    owners = owner_cell[0]
    slab_rows = flux_rows.shape[0]
    coarse_order = flux_rows.shape[1]
    live_rows = live_count[0, 0]
    position = lax.iota(jnp.int32, slab_rows)
    weights = (
        conductance[0]
        * (1 - clogged[0]).astype(jnp.float32)
        * (position < live_rows).astype(jnp.float32)
    ).astype(jnp.bfloat16)
    empty = jnp.zeros((coarse_order, coarse_order), jnp.float32)
    partial_value = accumulate(flux_rows, owners, weights, live_rows, empty)
    assembled = lax.psum(partial_value, "trans")
    face_row = coupling[0]
    leak_row = leakage[0]
    source_row = source[0]
    flux_diag = jnp.diagonal(assembled)
    schur_term = face_row * face_row / (face_row + leak_row + flux_diag)
    upstream = from_behind(jnp.stack([face_row, schur_term]), "flow", 1)
    face_before = upstream[0]
    diag_total = leak_row + face_row + face_before - upstream[1]
    system = assembled + jnp.diag(diag_total)
    pivots = 1.0 / jnp.diagonal(system)
    first_sweep = 2.0 * jnp.diag(pivots) - pivots[:, None] * system * pivots[None, :]
    band_rows = coarse_order // lax.axis_size("trans")
    row_start = lax.axis_index("trans") * band_rows
    first_band = lax.dynamic_slice_in_dim(first_sweep, row_start, band_rows, 0)
    left_product = jnp.dot(
        first_band, system, precision=lax.Precision.HIGHEST, preferred_element_type=jnp.float32
    )
    inverse_band = 2.0 * first_band - jnp.dot(
        left_product,
        first_sweep,
        precision=lax.Precision.HIGHEST,
        preferred_element_type=jnp.float32,
    )
    inverse_whole = lax.all_gather(inverse_band, "trans", axis=0, tiled=True)
    chain_turns = lax.axis_size("flow")
    flow_index = lax.axis_index("flow")
    zeros_full = jnp.zeros((coarse_order,), jnp.float32)

    def forward_turn(turn_index, carried):
        held, forward_state = carried
        received = from_behind(held, "flow", 1)

        def forward_active_turn():
            fresh = source_row + received
            return (face_row * matvec(inverse_whole, fresh), fresh)

        def forward_keep_turn():
            return (held, forward_state)

        return lax.cond(flow_index == turn_index, forward_active_turn, forward_keep_turn)

    unused, forward_state = lax.fori_loop(0, chain_turns, forward_turn, (zeros_full, zeros_full))

    def backward_turn(turn_index, held):
        received = from_behind(held, "flow", -1)

        def backward_active_turn():
            return matvec(inverse_whole, forward_state + face_row * received)

        def backward_keep_turn():
            return held

        return lax.cond(
            flow_index == chain_turns - 1 - turn_index, backward_active_turn, backward_keep_turn
        )

    pressure_full = lax.fori_loop(0, chain_turns, backward_turn, zeros_full)
    pressure_band = lax.dynamic_slice_in_dim(pressure_full, row_start, band_rows, 0)
    return pressure_band.reshape(1, band_rows)


def solution(mesh):
    placed = (
        P("flow", "trans", None),
        P("flow", "trans"),
        P("flow", "trans"),
        P("flow", "trans"),
        P("flow", "trans"),
        P("flow", None),
        P("flow", None),
        P("flow", None),
    )
    return jax.shard_map(
        per_device, mesh=mesh, in_specs=placed, out_specs=P("flow", "trans"), check_vma=False
    )
```

profile of v0, /device:TPU:8, one launch (start us, length us, event | category | flops | bytes accessed | tf_op | source)
XLA Modules:
  0.0 1608.5 jit_solution(6718076438722665603)
XLA Ops:
  15.5 89.7 %all-reduce.2.cloned.1.call-done = f32[1024,1024]{1,0:T(8,128)} async-done(((f32[1024,1024]{1,0:T(8,128)}), f32[1024,1024]{1,0:T(8,128)}) %all-reduce.2.cloned.1.call-update) | async-done | bytes 4194320 | tf_op jit(solution)/shard_map/psum | solution.py:55
  105.2 17.0 %gather_fusion = f32[1024]{0:T(1024)S(1)} fusion(f32[1024,1024]{1,0:T(8,128)} %all-reduce.2.cloned.1.call-done, s32[1024]{0:T(1024)S(1)} %bitcast.32), kind=kCustom, calls=%fused_computation | custom fusion | bytes 16384 | tf_op jit(solution)/shard_map/jit(diagonal)/cond/branch_0_fun/gather | solution.py:59
  131.9 17.1 %gather_fusion.1 = f32[1024]{0:T(1024)S(1)} fusion(f32[1024,1024]{1,0:T(8,128)} %select_add_fusion, s32[1024]{0:T(1024)S(1)} %bitcast.33), kind=kCustom, calls=%fused_computation.1 | custom fusion | bytes 16384 | tf_op jit(solution)/shard_map/jit(diagonal)/cond/branch_0_fun/gather | solution.py:65
  158.1 42.5 %all-gather.2.cloned.1.call-done = f32[1024,1024]{1,0:T(8,128)} async-done(((f32[128,1024]{1,0:T(8,128)}), f32[1024,1024]{1,0:T(8,128)}) %all-gather.2.cloned.1.call-update) | async-done | bytes 4194320 | tf_op jit(solution)/shard_map/all_gather | solution.py:79
  201.2 492.6 %while.42 = (s32[]{:T(128)}, f32[1024]{0:T(1024)S(1)}, f32[1024]{0:T(1024)}, s32[]{:T(128)}, f32[1024]{0:T(1024)S(1)}, /*index=5*/f32[1024,1024]{1,0:T(8,128)}, f32[1024]{0:T(1024)S(1)}, s32[]{:T(128)}) while((s32[]{:T(128)}, f32[1024]{0:T(1024)S(1)}, f32[1024]{0:T(1024)}, s32[]{:T(128)}, f32[1024]{0:T(1024)S(1)}, ...), condition=%wide.region_6.7_spmd, body=%wide.region_3.6_spmd.sunk | while | flops 12584964 | bytes 4243667 | solution.py:97
  214.8 10.4 collective-permute-start
  232.1 8.2 collective-permute-start
  247.0 8.2 collective-permute-start
  262.0 9.4 collective-permute-start
  279.4 7.0 collective-permute-start
  294.4 7.0 collective-permute-start
  309.4 7.0 collective-permute-start
  324.4 8.2 collective-permute-start
  340.6 7.0 collective-permute-start
  355.6 7.0 collective-permute-start
  370.6 7.0 collective-permute-start
  385.5 8.2 collective-permute-start
  401.7 7.0 collective-permute-start
  416.7 7.0 collective-permute-start
  431.7 7.0 collective-permute-start
  446.7 9.1 collective-permute-start
  510.3 6.6 collective-permute-start
  571.4 6.7 collective-permute-start
  632.6 6.6 collective-permute-start
  693.7 907.3 %while.43 = (s32[]{:T(128)}, f32[1024]{0:T(1024)S(1)}, s32[]{:T(128)}, f32[1024]{0:T(1024)S(1)}, f32[1024]{0:T(1024)}, /*index=5*/f32[1024,1024]{1,0:T(8,128)}, s32[]{:T(128)}, s32[]{:T(128)}) while((s32[]{:T(128)}, f32[1024]{0:T(1024)S(1)}, s32[]{:T(128)}, f32[1024]{0:T(1024)S(1)}, f32[1024]{0:T(1024)}, /*index=5*/f32[1024,1024]{1,0:T(8,128)}, ...), condition=%wide.region_10.11_spmd, body=%wide.region_7.10_spmd.sunk | while | flops 12584965 | bytes 4235455 | solution.py:112
  695.0 7.8 collective-permute-done.1
  704.1 6.6 collective-permute-done.1
  712.0 6.6 collective-permute-done.1
  719.9 6.6 collective-permute-done.1
  727.8 6.6 collective-permute-done.1
  743.5 6.6 collective-permute-done.1
  751.4 6.6 collective-permute-done.1
  759.2 6.9 collective-permute-done.1
  767.4 6.6 collective-permute-done.1
  783.1 6.6 collective-permute-done.1
  791.0 6.6 collective-permute-done.1
  798.9 6.6 collective-permute-done.1
  806.7 6.6 collective-permute-done.1
  814.6 6.6 collective-permute-done.1
  822.5 6.9 collective-permute-done.1
  830.7 6.6 collective-permute-done.1
  846.4 6.6 collective-permute-done.1
  862.1 6.6 collective-permute-done.1
  870.0 6.6 collective-permute-done.1
  877.9 6.6 collective-permute-done.1
  885.8 6.9 collective-permute-done.1
  894.0 6.6 collective-permute-done.1
  909.7 6.6 collective-permute-done.1
  933.3 6.6 collective-permute-done.1
  949.0 7.9 collective-permute-done.1
  973.9 6.6 collective-permute-done.1
  997.5 6.6 collective-permute-done.1
  1013.2 6.9 collective-permute-done.1
  1021.4 6.6 collective-permute-done.1
  1037.2 6.6 collective-permute-done.1
  1060.8 6.6 collective-permute-done.1
  1076.5 6.9 collective-permute-done.1
  1092.3 6.6 collective-permute-done.1
  1107.8 6.6 collective-permute-done.1
  1123.3 6.6 collective-permute-done.1
  1138.8 7.8 collective-permute-done.1
  1155.6 6.6 collective-permute-done.1
  1171.1 6.7 collective-permute-done.1
  1194.2 400.5 %collective-permute-done.1 = f32[1024]{0:T(1024)S(1)} collective-permute-done((f32[1024]{0:T(1024)S(1)}, f32[1024]{0:T(1024)S(1)}, u32[]{:S(2)}, u32[]{:S(2)}) %collective-permute-start.1) | collective-permute-done | bytes 4128 | tf_op jit(solution)/shard_map/while/body/eval_jaxpr/ppermute | solution.py:12
  (367 shorter events, 643.2 us)
Async XLA Ops:
  6.5 98.7 %all-reduce.2.cloned.1.call-start = ((), (), s32[]{:S(2)}) async-start(), calls=%async_computation | async-start | bytes 8388608 | tf_op jit(solution)/shard_map/psum | solution.py:55
  15.4 185.2 %all-gather.2.cloned.1.call-start = ((), (), s32[]{:S(2)}) async-start(), calls=%async_computation.1 | async-start | bytes 4718592 | tf_op jit(solution)/shard_map/all_gather | solution.py:79
  214.8 11.8 collective-permute-start
  232.1 9.5 collective-permute-start
  247.0 9.5 collective-permute-start
  262.0 10.7 collective-permute-start
  279.4 8.3 collective-permute-start
  294.4 8.3 collective-permute-start
  309.4 8.3 collective-permute-start
  324.4 9.5 collective-permute-start
  340.6 8.3 collective-permute-start
  355.6 8.3 collective-permute-start
  370.6 8.3 collective-permute-start
  385.5 9.5 collective-permute-start
  401.7 8.3 collective-permute-start
  416.7 8.3 collective-permute-start
  431.7 8.3 collective-permute-start
  446.7 10.4 collective-permute-start
  510.3 7.9 collective-permute-start
  571.4 8.0 collective-permute-start
  632.6 7.9 collective-permute-start
  693.7 9.1 collective-permute-start.1
  702.8 7.9 collective-permute-start.1
  710.7 7.9 collective-permute-start.1
  718.6 7.9 collective-permute-start.1
  726.5 7.9 collective-permute-start.1
  734.3 7.9 collective-permute-start.1
  742.2 7.9 collective-permute-start.1
  750.1 7.9 collective-permute-start.1
  757.9 8.2 collective-permute-start.1
  766.1 7.9 collective-permute-start.1
  774.0 7.9 collective-permute-start.1
  781.8 7.9 collective-permute-start.1
  789.7 7.9 collective-permute-start.1
  797.6 7.9 collective-permute-start.1
  805.4 7.9 collective-permute-start.1
  813.3 7.9 collective-permute-start.1
  821.2 8.2 collective-permute-start.1
  829.4 7.9 collective-permute-start.1
  837.3 7.9 collective-permute-start.1
  845.1 7.9 collective-permute-start.1
  860.8 7.9 collective-permute-start.1
  868.7 7.9 collective-permute-start.1
  876.6 7.9 collective-permute-start.1
  884.5 8.2 collective-permute-start.1
  892.7 7.9 collective-permute-start.1
  900.5 7.9 collective-permute-start.1
  908.4 7.9 collective-permute-start.1
  932.0 7.9 collective-permute-start.1
  947.7 9.2 collective-permute-start.1
  972.6 7.9 collective-permute-start.1
  996.2 7.9 collective-permute-start.1
  1011.9 8.2 collective-permute-start.1
  1020.1 7.9 collective-permute-start.1
  1035.9 7.9 collective-permute-start.1
  1059.5 7.9 collective-permute-start.1
  1075.2 8.2 collective-permute-start.1
  1091.0 7.9 collective-permute-start.1
  1106.5 7.9 collective-permute-start.1
  1122.0 7.9 collective-permute-start.1
  1137.5 9.1 collective-permute-start.1
  1154.3 7.9 collective-permute-start.1
  1169.8 8.0 collective-permute-start.1
  1192.9 401.8 %collective-permute-start.1 = (f32[1024]{0:T(1024)S(1)}, f32[1024]{0:T(1024)S(1)}, u32[]{:S(2)}, u32[]{:S(2)}) collective-permute-start(f32[1024]{0:T(1024)S(1)} %get-tuple-element.536), channel_id=1, source_target_pairs={{8,0},{16,8},{24,16},{32,24},{40,32},{48,40},{56,48},{64,56},{72,6... | collective-permute-start | bytes 12296 | tf_op jit(solution)/shard_map/while/body/eval_jaxpr/ppermute | solution.py:12
  (73 other events, 755.8 us)
Sparse Core Ops, SparseCore 0:
  15.5 89.6 all-reduce.1
  158.2 42.3 all-gather.1
where the time goes:
time: 1620 us; the launch traced here: 1610 us
  waiting for transfers between devices  1040 us (64%)
  starting transfers between devices  487 us (30%)
  local copies, waits for them, and re-layouts  37.9 us (2%)
  matrix products  21.9 us (1%)
    ppermute x129, waiting for transfers between devices, from_behind(): lax.ppermute(value, axis, [(source, source + steps) for source in range(i...  903 us
    ppermute x129, starting transfers between devices, from_behind(): lax.ppermute(value, axis, [(source, source + steps) for source in range(i...  487 us
    psum x1, waiting for transfers between devices, per_device(): assembled = lax.psum(partial_value, 'trans')  89.7 us
    all_gather x1, waiting for transfers between devices, per_device(): inverse_whole = lax.all_gather(inverse_band, 'trans', axis=0, tiled=True)  42.5 us
  transfers between devices with their start and end apart: 131, of which 131 were waited for; matrix products, arithmetic and copies ran while one was open for 0% of the time, Pallas kernels for 0%

commit v1 on v0

v1 whole, which is shorter than its diff:
```python
import functools

import jax
import jax.numpy as jnp
from jax import lax
from jax.experimental import pallas as pl
from jax.experimental.pallas import tpu as pltpu
from jax.sharding import PartitionSpec as P

MESH = pl.DeviceIdType.MESH
BF16 = jnp.bfloat16
F32 = jnp.float32
VMEM_LIMIT = 56 * 1024 * 1024


def dot(left, right):
    return jnp.dot(left, right, preferred_element_type=F32)


def split(value):
    high = value.astype(BF16)
    return high, (value - high.astype(F32)).astype(BF16)


def neighbours(plane, planes):
    return jnp.where(plane > 0, 1, 0) + jnp.where(plane < planes - 1, 1, 0)


def setup_kernel(
    planes, chips, rows, order,
    basis, owner, clogged, conductance, live, coupling, leakage,
    near_high, near_low, inverse_diag,
    slabs, packs, picked, block, gain_high, gain_low, square, faces, faces_in, flux_diag,
    slab_send, slab_recv, pack_send, pack_recv, face_send, face_recv,
):
    plane = lax.axis_index("flow")
    me = lax.axis_index("trans")
    parts = 2 * chips
    chip, core = me // 2, lax.rem(me, 2)
    partner = chip * 2 + 1 - core
    step_rows = 256
    steps = order // step_rows

    barrier = pltpu.get_barrier_semaphore()
    for turn in range(1, parts):
        pl.semaphore_signal(
            barrier, inc=1, device_id=(plane, lax.rem(me + turn, parts)), device_id_type=MESH
        )

    @pl.when(plane > 0)
    def _():
        pl.semaphore_signal(barrier, inc=1, device_id=(plane - 1, me), device_id_type=MESH)

    @pl.when(plane < planes - 1)
    def _():
        pl.semaphore_signal(barrier, inc=1, device_id=(plane + 1, me), device_id_type=MESH)

    def slab(index):
        return slabs.at[:, pl.ds(pl.multiple_of(index * rows, rows), rows)]

    position = lax.broadcasted_iota(jnp.int32, (1, rows), 1)
    weight = (
        conductance[...]
        * (1 - clogged[...]).astype(F32)
        * (position < live[...]).astype(F32)
    ).astype(BF16).astype(F32)
    row_id = lax.broadcasted_iota(jnp.int32, (8, rows), 0)
    packs[me] = jnp.where(row_id == 0, weight, owner[...].astype(F32))
    slabs[:, pl.ds(pl.multiple_of(me * rows, rows), rows)] = basis[0].astype(F32).T.astype(BF16)

    pl.semaphore_wait(barrier, parts - 1 + neighbours(plane, planes))

    def slab_copy(index, target, slot):
        return pltpu.make_async_remote_copy(
            slab(index), slab(index), slab_send.at[slot], slab_recv.at[index],
            device_id=(plane, target), device_id_type=MESH,
        )

    def pack_copy(index, target, slot):
        return pltpu.make_async_remote_copy(
            packs.at[index], packs.at[index], pack_send.at[slot], pack_recv.at[index],
            device_id=(plane, target), device_id_type=MESH,
        )

    others = [lax.rem(me + turn, parts) for turn in range(1, parts)]
    for slot, target in enumerate(others):
        pack_copy(me, target, slot).start()
    away = [lax.rem(chip + turn, chips) * 2 + core for turn in (1, chips - 1, *range(2, chips - 1))]
    for slot, target in enumerate(away):
        slab_copy(me, target, slot).start()
    slab_copy(me, partner, chips - 1).start()

    column = lax.broadcasted_iota(jnp.int32, (rows, order), 1).astype(F32)

    def pick(index, carry):
        turned = packs[index].T
        picked[pl.ds(pl.multiple_of(index * rows, rows), rows), :] = jnp.where(
            turned[:, 1:2] == column, turned[:, 0:1], 0.0
        ).astype(BF16)
        return carry

    for source in others:
        pack_copy(source, partner, 0).wait_recv()
    lax.fori_loop(0, parts, pick, 0)

    for slot, source in enumerate(away):
        slab_copy(source, partner, 0).wait_recv()
        slab_copy(source, partner, chips + slot).start()
    slab_copy(partner, partner, 0).wait_recv()
    for source in away:
        slab_copy(source + 1 - 2 * core, partner, 0).wait_recv()

    eye = lax.broadcasted_iota(jnp.int32, (rows, rows), 0) == lax.broadcasted_iota(
        jnp.int32, (rows, rows), 1
    )
    for index in range(order // rows):
        here = pl.ds(index * rows, rows)
        flux_diag[:, here] = jnp.sum(
            jnp.where(eye, dot(slabs[here, :], picked[:, here]), 0.0), axis=0, keepdims=True
        )

    face = coupling[...]
    leak = leakage[...]
    schur = face * face / (face + leak + flux_diag[...])
    faces[0:1, :] = face
    faces[1:2, :] = schur

    def face_copy(target):
        return pltpu.make_async_remote_copy(
            faces, faces_in, face_send, face_recv, device_id=(target, me), device_id_type=MESH
        )

    @pl.when(plane < planes - 1)
    def _():
        face_copy(plane + 1).start()

    def assemble(index, carry):
        here = pl.ds(pl.multiple_of(index * step_rows, step_rows), step_rows)
        block[here, :] = dot(slabs[here, :], picked[...])
        return carry

    lax.fori_loop(0, steps, assemble, 0)

    @pl.when(plane > 0)
    def _():
        face_copy(plane).wait_recv()

    @pl.when(plane == 0)
    def _():
        faces_in[...] = jnp.zeros_like(faces_in)

    diag = flux_diag[...] + (leak + face + faces_in[0:1, :] - faces_in[1:2, :])
    pivots = 1.0 / diag
    inverse_diag[...] = pivots

    across = lax.broadcasted_iota(jnp.int32, (step_rows, order), 1)
    down = lax.broadcasted_iota(jnp.int32, (step_rows, order), 0)

    def scale(index, carry):
        here = pl.ds(pl.multiple_of(index * step_rows, step_rows), step_rows)
        gain = jnp.where(across == down + index * step_rows, 0.0, block[here, :] * pivots)
        block[here, :] = gain
        gain_high[here, :], gain_low[here, :] = split(gain)
        return carry

    lax.fori_loop(0, steps, scale, 0)

    def squared(index, carry):
        here = pl.ds(pl.multiple_of(index * step_rows, step_rows), step_rows)
        high, low = gain_high[here, :], gain_low[here, :]
        value = dot(high, gain_high[...]) + (dot(high, gain_low[...]) + dot(low, gain_high[...]))
        square[here, :] = value.astype(BF16)
        block[here, :] = value - block[here, :]
        return carry

    lax.fori_loop(0, steps, squared, 0)

    def finish(index, carry):
        here = pl.ds(pl.multiple_of(index * step_rows, step_rows), step_rows)
        near = block[here, :] - dot(gain_high[here, :], square[...])
        near_high[here, :], near_low[here, :] = split(near)
        return carry

    lax.fori_loop(0, steps, finish, 0)

    for slot, target in enumerate(others):
        pack_copy(me, target, slot).wait_send()
    for slot, target in enumerate(away):
        slab_copy(me, target, slot).wait_send()
        slab_copy(target, partner, chips + slot).wait_send()
    slab_copy(me, partner, chips - 1).wait_send()

    @pl.when(plane < planes - 1)
    def _():
        face_copy(plane + 1).wait_send()


def chain_kernel(
    planes, rows, order,
    near_high, near_low, inverse_diag, coupling, source,
    pressure,
    level, sent, received, answer, band_in, send_sem, recv_sem, band_send, band_recv,
):
    plane = lax.axis_index("flow")
    me = lax.axis_index("trans")
    core = lax.rem(me, 2)
    partner = me + 1 - 2 * core
    row_id = lax.broadcasted_iota(jnp.int32, (8, order), 0)

    def apply(value):
        scaled = value * inverse_diag[...]
        high, low = split(scaled)
        both = jnp.where(
            row_id == 0, high.astype(F32), jnp.where(row_id == 1, low.astype(F32), 0.0)
        ).astype(BF16)
        gathered = dot(both, near_high[...]) + dot(both, near_low[...])
        return scaled + jnp.sum(gathered, axis=0, keepdims=True)

    barrier = pltpu.get_barrier_semaphore()
    pl.semaphore_signal(barrier, inc=1, device_id=(plane, partner), device_id_type=MESH)

    def step_copy(way, target):
        return pltpu.make_async_remote_copy(
            sent.at[way], received.at[way], send_sem.at[way], recv_sem.at[way],
            device_id=(target, me), device_id_type=MESH,
        )

    band_copy = pltpu.make_async_remote_copy(
        answer.at[:, pl.ds(pl.multiple_of(partner * rows, rows), rows)], band_in,
        band_send, band_recv, device_id=(plane, partner), device_id_type=MESH,
    )

    @pl.when(core == 0)
    def _():
        pl.semaphore_wait(barrier, 1)
        band_copy.wait_recv()
        pressure[...] = band_in[...]

    @pl.when(core == 1)
    def _():
        @pl.when(plane > 0)
        def _():
            pl.semaphore_signal(barrier, inc=1, device_id=(plane - 1, me), device_id_type=MESH)

        @pl.when(plane < planes - 1)
        def _():
            pl.semaphore_signal(barrier, inc=1, device_id=(plane + 1, me), device_id_type=MESH)

        pl.semaphore_wait(barrier, 1 + neighbours(plane, planes))

        level[...] = source[...]

        @pl.when(plane > 0)
        def _():
            step_copy(0, plane).wait_recv()
            level[...] = source[...] + received[0]

        @pl.when(plane < planes - 1)
        def _():
            sent[0] = coupling[...] * apply(level[...])
            step_copy(0, plane + 1).start()
            step_copy(1, plane).wait_recv()
            level[...] = level[...] + coupling[...] * received[1]

        answer[...] = apply(level[...])

        @pl.when(plane > 0)
        def _():
            sent[1] = answer[...]
            step_copy(1, plane - 1).start()

        band_copy.start()
        pressure[...] = answer[:, pl.ds(pl.multiple_of(me * rows, rows), rows)]

        @pl.when(plane < planes - 1)
        def _():
            step_copy(0, plane + 1).wait_send()

        @pl.when(plane > 0)
        def _():
            step_copy(1, plane - 1).wait_send()

        band_copy.wait_send()


def per_device(basis_flux, owner_cell, clogged, conductance, live_count, coupling, leakage, source):
    planes = lax.axis_size("flow")
    parts = lax.axis_size("trans")
    chips = parts // 2
    rows, order = basis_flux.shape[1:]
    vmem = pl.BlockSpec(memory_space=pltpu.VMEM)
    dma = pltpu.SemaphoreType.DMA
    matrix = jax.ShapeDtypeStruct((order, order), BF16)
    near_high, near_low, inverse_diag = pl.pallas_call(
        functools.partial(setup_kernel, planes, chips, rows, order),
        out_shape=(matrix, matrix, jax.ShapeDtypeStruct((1, order), F32)),
        in_specs=[vmem] * 7,
        out_specs=(vmem,) * 3,
        scratch_shapes=[
            pltpu.VMEM((order, parts * rows), BF16),
            pltpu.VMEM((parts, 8, rows), F32),
            pltpu.VMEM((parts * rows, order), BF16),
            pltpu.VMEM((order, order), F32),
            pltpu.VMEM((order, order), BF16),
            pltpu.VMEM((order, order), BF16),
            pltpu.VMEM((order, order), BF16),
            pltpu.VMEM((2, order), F32),
            pltpu.VMEM((2, order), F32),
            pltpu.VMEM((1, order), F32),
            dma((parts,)), dma((parts,)), dma((parts,)), dma((parts,)), dma, dma,
        ],
        compiler_params=pltpu.CompilerParams(
            collective_id=0, has_side_effects=True, vmem_limit_bytes=VMEM_LIMIT
        ),
    )(basis_flux, owner_cell, clogged, conductance, live_count, coupling, leakage)
    return pl.pallas_call(
        functools.partial(chain_kernel, planes, rows, order),
        out_shape=jax.ShapeDtypeStruct((1, rows), F32),
        in_specs=[vmem] * 5,
        out_specs=vmem,
        scratch_shapes=[
            pltpu.VMEM((1, order), F32),
            pltpu.VMEM((2, 1, order), F32),
            pltpu.VMEM((2, 1, order), F32),
            pltpu.VMEM((1, order), F32),
            pltpu.VMEM((1, rows), F32),
            dma((2,)), dma((2,)), dma, dma,
        ],
        compiler_params=pltpu.CompilerParams(
            collective_id=1, has_side_effects=True, vmem_limit_bytes=VMEM_LIMIT
        ),
    )(near_high, near_low, inverse_diag, coupling, source)


def solution(mesh):
    placed = (
        P("flow", "trans", None),
        P("flow", "trans"),
        P("flow", "trans"),
        P("flow", "trans"),
        P("flow", "trans"),
        P("flow", None),
        P("flow", None),
        P("flow", None),
    )
    return jax.shard_map(
        per_device, mesh=mesh, in_specs=placed, out_specs=P("flow", "trans"), check_vma=False
    )
```

time: 1620 us -> 373 us (0.23)
  the two profiles are of different devices: /device:TPU:8 before, /device:TPU:1 now
where the time goes in v1:
time: 373 us
  Pallas kernels  371 us (99%)
    pallas_call x1, Pallas kernels, per_device(): pl.pallas_call(functools.partial(chain_kernel, planes, rows, order), out_...  328 us
    pallas_call x1, Pallas kernels, per_device(): pl.pallas_call(functools.partial(setup_kernel, planes, chips, rows, order...  43 us

profile of v1, /device:TPU:1, one launch (start us, length us, event | category | flops | bytes accessed | tf_op | source)
XLA Modules:
  0.0 373.1 jit_solution(8590728914663913159)
XLA Ops:
  0.7 43.0 %shard_map.82 = (bf16[1024,1024]{1,0:T(8,128)(2,1)}, bf16[1024,1024]{1,0:T(8,128)(2,1)}, f32[1,1024]{1,0:T(1,128)}) custom-call(bf16[1,128,1024]{2,1,0:T(8,128)(2,1)} %basis.1, s32[1,128]{1,0:T(1,128)} %owner.1, s32[1,128]{1,0:T(1,128)} %clogged.1, f32[1,128]{1,0:T(1,128)} %conductance.1, s32[1,1]{1,0:T(1,128)S(6)} %copy.10.live, f32[1,1024]{1,0:T(1,128)} %coupling.3, ...), custom_call_target="tpu_custom_call" | custom-call | tf_op jit(solution)/shard_map/pallas_call | solution.py:294
  43.6 328.3 %shard_map.83 = f32[1,128]{1,0:T(1,128)} custom-call(bf16[1024,1024]{1,0:T(8,128)(2,1)} %get-tuple-element.8.near_high, bf16[1024,1024]{1,0:T(8,128)(2,1)} %get-tuple-element.9.near_low, f32[1,1024]{1,0:T(1,128)} %get-tuple-element.10.inverse_diag, f32[1,1024]{1,0:T(1,128)} %coupling.3, f32[1,1024]{1,0:T(1,128)} %source.1), custom_call_target="tpu_custom_call" | custom-call | tf_op jit(solution)/shard_map/pallas_call | solution.py:316
  371.9 1.2 copy.11

commit v2 on v1

--- a/solution.py
+++ b/solution.py
@@ -196,89 +196,407 @@
 
 
 def chain_kernel(
-    planes, rows, order,
+    planes, span, chips, rows, order, depth,
     near_high, near_low, inverse_diag, coupling, source,
     pressure,
-    level, sent, received, answer, band_in, send_sem, recv_sem, band_send, band_recv,
+    panel_in, panel_out, back_in, back_out, back_held,
+    panel_high, panel_low, last_high, last_low, back_high, back_low,
+    level, parts_out, level_out, level_in, up_pieces, down_pieces, end_pieces, end_out,
+    edge_up, edge_down, swept_in, swept, band_out, band_in,
+    panel_send, panel_recv, held_send, held_recv, up_send, up_recv, down_send, down_recv,
+    edge_send, edge_recv, level_send, level_recv, sweep_send, sweep_recv,
+    end_send, end_recv, band_send, band_recv,
 ):
     plane = lax.axis_index("flow")
     me = lax.axis_index("trans")
-    core = lax.rem(me, 2)
+    chip, core = me // 2, lax.rem(me, 2)
     partner = me + 1 - 2 * core
-    row_id = lax.broadcasted_iota(jnp.int32, (8, order), 0)
+    spans = planes // span
+    row, spot = plane // span, lax.rem(plane, span)
+    row_start = row * span
+    last = span - 1
+    width = order // chips
+    turns = width // depth
+    wide = width // rows
+    first_column = pl.multiple_of(chip * width, width)
+    face = coupling[...]
+    other_chips = [lax.rem(chip + turn, chips) for turn in range(1, chips)]
+
+    def remote(source_ref, target_ref, send, recv, target_plane, target):
+        return pltpu.make_async_remote_copy(
+            source_ref, target_ref, send, recv,
+            device_id=(target_plane, target), device_id_type=MESH,
+        )
 
     def apply(value):
+        count = value.shape[0]
         scaled = value * inverse_diag[...]
-        high, low = split(scaled)
-        both = jnp.where(
-            row_id == 0, high.astype(F32), jnp.where(row_id == 1, low.astype(F32), 0.0)
-        ).astype(BF16)
-        gathered = dot(both, near_high[...]) + dot(both, near_low[...])
-        return scaled + jnp.sum(gathered, axis=0, keepdims=True)
+        high = scaled.astype(BF16).astype(F32)
+        both = jnp.concatenate([high, scaled - high], axis=0).astype(BF16)
+        by_high = dot(both, near_high[...])
+        by_low = dot(high.astype(BF16), near_low[...])
+        return scaled + (by_high[:count] + (by_high[count:] + by_low))
+
+    def two_rows(value):
+        row_id = lax.broadcasted_iota(jnp.int32, (8, value.shape[1]), 0)
+        high = value.astype(BF16).astype(F32)
+        return jnp.where(row_id == 0, high, jnp.where(row_id == 1, value - high, 0.0)).astype(BF16)
+
+    def apply_one(value):
+        scaled = value * inverse_diag[...]
+        both = two_rows(scaled)
+        return scaled + jnp.sum(
+            dot(both, near_high[...]) + dot(both, near_low[...]), axis=0, keepdims=True
+        )
+
+    def by_panel(value, high, low):
+        both = two_rows(value)
+        return jnp.sum(dot(both, high[...]) + dot(both, low[...]), axis=0, keepdims=True)
+
+    def take(index):
+        return pl.ds(pl.multiple_of(index * depth, depth), depth)
 
     barrier = pltpu.get_barrier_semaphore()
-    pl.semaphore_signal(barrier, inc=1, device_id=(plane, partner), device_id_type=MESH)
-
-    def step_copy(way, target):
-        return pltpu.make_async_remote_copy(
-            sent.at[way], received.at[way], send_sem.at[way], recv_sem.at[way],
-            device_id=(target, me), device_id_type=MESH,
-        )
-
-    band_copy = pltpu.make_async_remote_copy(
-        answer.at[:, pl.ds(pl.multiple_of(partner * rows, rows), rows)], band_in,
-        band_send, band_recv, device_id=(plane, partner), device_id_type=MESH,
-    )
+
+    def greet(target_plane, target):
+        pl.semaphore_signal(barrier, inc=1, device_id=(target_plane, target), device_id_type=MESH)
+
+    greet(plane, partner)
+    inner = jnp.where(spot > 0, 1, 0) + jnp.where(spot < last, 1, 0)
 
     @pl.when(core == 0)
     def _():
-        pl.semaphore_wait(barrier, 1)
+        @pl.when(spot > 0)
+        def _():
+            greet(plane - 1, me)
+
+        @pl.when(spot < last)
+        def _():
+            greet(plane + 1, me)
+
+        pl.semaphore_wait(barrier, 1 + inner)
+
+    at_end = jnp.logical_or(spot == 0, spot == last)
+
+    @pl.when(core == 1)
+    def _():
+        for other in other_chips:
+            greet(plane, other * 2 + 1)
+
+        for place in range(span):
+            if place in (0, last):
+                meets = spot != place
+            else:
+                meets = jnp.logical_or(at_end, jnp.abs(spot - place) == 1)
+                meets = jnp.logical_and(meets, spot != place)
+
+            @pl.when(meets)
+            def _():
+                greet(row_start + place, me)
+
+        for step, there in ((span, row < spans - 1), (-span, row > 0)):
+            @pl.when(jnp.logical_and(at_end, there))
+            def _():
+                for other in range(chips):
+                    greet(plane + step, other * 2 + 1)
+
+        beside = jnp.logical_or(spot == 1, spot == last - 1)
+        along = jnp.where(at_end, last, jnp.where(beside, 3, 4))
+        across = jnp.where(row > 0, chips, 0) + jnp.where(row < spans - 1, chips, 0)
+        pl.semaphore_wait(barrier, chips + along + jnp.where(at_end, across, 0))
+
+    one_hot_row = lax.broadcasted_iota(jnp.int32, (depth, order), 0)
+    one_hot_column = lax.broadcasted_iota(jnp.int32, (depth, order), 1)
+
+    def unit_rows(index):
+        return jnp.where(
+            one_hot_column == one_hot_row + (chip * width + index * depth), 1.0, 0.0
+        )
+
+    def back_copy(index):
+        return remote(
+            back_out.at[take(index), :], back_in.at[take(index), :],
+            panel_send.at[index], panel_recv.at[index], plane - 1, me,
+        )
+
+    def held_copy(index):
+        return remote(
+            back_out.at[take(index), :], back_held.at[take(index), :],
+            held_send.at[index], held_recv.at[index], plane, partner,
+        )
+
+    band_copy = remote(band_out, band_in, band_send, band_recv, plane, partner)
+
+    @pl.when(core == 0)
+    def _():
+        def flow(index, carry):
+            @pl.when(spot == last)
+            def _():
+                back_in[take(index), :] = unit_rows(index)
+
+            @pl.when(spot < last)
+            def _():
+                back_copy(index).wait_recv()
+
+            back_out[take(index), :] = apply(face * back_in[take(index), :])
+
+            @pl.when(spot > 0)
+            def _():
+                back_copy(index).start()
+
+            held_copy(index).start()
+            return carry
+
+        lax.fori_loop(0, turns, flow, 0)
+
+        def drain(index, carry):
+            @pl.when(spot > 0)
+            def _():
+                back_copy(index).wait_send()
+
+            held_copy(index).wait_send()
+            return carry
+
+        lax.fori_loop(0, turns, drain, 0)
         band_copy.wait_recv()
         pressure[...] = band_in[...]
 
+    def panel_copy(index):
+        return remote(
+            panel_out.at[take(index), :], panel_in.at[take(index), :],
+            panel_send.at[index], panel_recv.at[index], plane + 1, me,
+        )
+
+    def up_copy(target):
+        return remote(
+            parts_out.at[target], up_pieces.at[chip],
+            up_send.at[target], up_recv.at[chip], plane + span, target * 2 + 1,
+        )
+
+    def down_copy(target):
+        return remote(
+            parts_out.at[target], down_pieces.at[chip],
+            down_send.at[target], down_recv.at[chip], plane - span, target * 2 + 1,
+        )
+
+    def edge_copy(way, ref, place):
+        return remote(
+            ref, ref, edge_send.at[way, place], edge_recv.at[way], row_start + place, me
+        )
+
+    def level_copy(target, slot):
+        return remote(
+            level_out, level_in.at[chip], level_send.at[slot], level_recv.at[chip],
+            plane, target * 2 + 1,
+        )
+
+    def end_copy(target, slot):
+        return remote(
+            end_out.at[target], end_pieces.at[chip], end_send.at[slot], end_recv.at[chip],
+            plane, target * 2 + 1,
+        )
+
+    sweep_copy = remote(swept, swept_in, sweep_send, sweep_recv, plane - 1, me)
+
+    def cut(value, ref):
+        for index in range(chips):
+            ref[index] = value[:, index * width : (index + 1) * width]
+
     @pl.when(core == 1)
     def _():
-        @pl.when(plane > 0)
-        def _():
-            pl.semaphore_signal(barrier, inc=1, device_id=(plane - 1, me), device_id_type=MESH)
-
-        @pl.when(plane < planes - 1)
-        def _():
-            pl.semaphore_signal(barrier, inc=1, device_id=(plane + 1, me), device_id_type=MESH)
-
-        pl.semaphore_wait(barrier, 1 + neighbours(plane, planes))
-
-        level[...] = source[...]
-
-        @pl.when(plane > 0)
-        def _():
-            step_copy(0, plane).wait_recv()
-            level[...] = source[...] + received[0]
-
-        @pl.when(plane < planes - 1)
-        def _():
-            sent[0] = coupling[...] * apply(level[...])
-            step_copy(0, plane + 1).start()
-            step_copy(1, plane).wait_recv()
-            level[...] = level[...] + coupling[...] * received[1]
-
-        answer[...] = apply(level[...])
-
-        @pl.when(plane > 0)
-        def _():
-            sent[1] = answer[...]
-            step_copy(1, plane - 1).start()
-
+        def flow(turn, carry):
+            index = lax.rem(turn + turns, turns + 1)
+
+            @pl.when(spot == 0)
+            def _():
+                panel_in[take(index), :] = unit_rows(index)
+
+            @pl.when(spot > 0)
+            def _():
+                panel_copy(index).wait_recv()
+
+            @pl.when(turn == 0)
+            def _():
+                @pl.when(spot == 0)
+                def _():
+                    panel_in[take(index), :] = jnp.zeros((depth, order), F32)
+
+                panel_in[take(index), :] = panel_in[take(index), :] + jnp.where(
+                    one_hot_row == 0, source[...], 0.0
+                )
+
+            panel_out[take(index), :] = face * apply(panel_in[take(index), :])
+
+            @pl.when(spot < last)
+            def _():
+                panel_copy(index).start()
+
+            return carry
+
+        lax.fori_loop(0, turns + 1, flow, 0)
+        panel_high[...], panel_low[...] = split(panel_in[0:width, :])
+        level[...] = panel_in[width : width + 1, :]
+
+        @pl.when(spot == last)
+        def _():
+            last_high[...], last_low[...] = split(panel_out[0:width, :])
+
+            @pl.when(row > 0)
+            def _():
+                for target in range(chips):
+                    remote(
+                        parts_out.at[target], up_pieces.at[target],
+                        up_send.at[target], up_recv.at[target], plane, me,
+                    ).wait_recv()
+                edge_up[...] = (up_pieces[0] + up_pieces[1]) + (up_pieces[2] + up_pieces[3])
+
+            @pl.when(row == 0)
+            def _():
+                edge_up[...] = jnp.zeros_like(edge_up)
+
+            @pl.when(row < spans - 1)
+            def _():
+                cut(by_panel(edge_up[...], last_high, last_low), parts_out)
+                parts_out[chip] = parts_out[chip] + panel_out[
+                    width : width + 1, pl.ds(first_column, width)
+                ]
+                for target in range(chips):
+                    up_copy(target).start()
+
+            @pl.when(row > 0)
+            def _():
+                for place in range(last - 1, -1, -1):
+                    edge_copy(0, edge_up, place).start()
+
+        @pl.when(row > 0)
+        def _():
+            @pl.when(spot < last)
+            def _():
+                edge_copy(0, edge_up, 0).wait_recv()
+
+            level_out[...] = by_panel(edge_up[...], panel_high, panel_low)
+            for slot, other in enumerate(other_chips):
+                level_copy(other, slot).start()
+            level_in[chip] = level_out[...]
+            for other in other_chips:
+                remote(
+                    level_out, level_in.at[other], level_send.at[0], level_recv.at[other],
+                    plane, me,
+                ).wait_recv()
+            level[...] = level[...] + ((level_in[0] + level_in[1]) + (level_in[2] + level_in[3]))
+
+        @pl.when(spot < last)
+        def _():
+            sweep_copy.wait_recv()
+            level[...] = level[...] + face * swept_in[...]
+
+        swept[...] = apply_one(level[...])
+
+        @pl.when(spot > 0)
+        def _():
+            sweep_copy.start()
+
+        def arrived(index, carry):
+            held_copy(index).wait_recv()
+            return carry
+
+        lax.fori_loop(0, turns, arrived, 0)
+        back_high[...], back_low[...] = split(back_held[...])
+
+        @pl.when(jnp.logical_and(spot == last, row < spans - 1))
+        def _():
+            for target in range(chips):
+                up_copy(target).wait_send()
+
+        @pl.when(spot == 0)
+        def _():
+            @pl.when(row < spans - 1)
+            def _():
+                for target in range(chips):
+                    remote(
+                        parts_out.at[target], down_pieces.at[target],
+                        down_send.at[target], down_recv.at[target], plane, me,
+                    ).wait_recv()
+                edge_down[...] = (down_pieces[0] + down_pieces[1]) + (
+                    down_pieces[2] + down_pieces[3]
+                )
+
+            @pl.when(row == spans - 1)
+            def _():
+                edge_down[...] = jnp.zeros_like(edge_down)
+
+            @pl.when(row > 0)
+            def _():
+                cut(by_panel(edge_down[...], back_high, back_low), parts_out)
+                parts_out[chip] = parts_out[chip] + swept[:, pl.ds(first_column, width)]
+                for target in range(chips):
+                    down_copy(target).start()
+
+            @pl.when(row < spans - 1)
+            def _():
+                for place in range(1, span):
+                    edge_copy(1, edge_down, place).start()
+
+        end_pieces[chip] = jnp.zeros((1, width), F32)
+
+        @pl.when(row < spans - 1)
+        def _():
+            @pl.when(spot > 0)
+            def _():
+                edge_copy(1, edge_down, 0).wait_recv()
+
+            cut(by_panel(edge_down[...], back_high, back_low), end_out)
+            for slot, other in enumerate(other_chips):
+                end_copy(other, slot).start()
+            end_pieces[chip] = end_out[chip]
+            for other in other_chips:
+                remote(
+                    end_out.at[other], end_pieces.at[other], end_send.at[0], end_recv.at[other],
+                    plane, me,
+                ).wait_recv()
+            end_pieces[chip] = (end_pieces[0] + end_pieces[1]) + (end_pieces[2] + end_pieces[3])
+
+        answer = end_pieces[chip] + swept[:, pl.ds(first_column, width)]
+        band_out[...] = answer[:, 0:rows]
         band_copy.start()
-        pressure[...] = answer[:, pl.ds(pl.multiple_of(me * rows, rows), rows)]
-
-        @pl.when(plane < planes - 1)
-        def _():
-            step_copy(0, plane + 1).wait_send()
-
-        @pl.when(plane > 0)
-        def _():
-            step_copy(1, plane - 1).wait_send()
+        pressure[...] = answer[:, rows:width]
+
+        @pl.when(spot < last)
+        def _():
+            def drain(index, carry):
+                panel_copy(index).wait_send()
+                return carry
+
+            lax.fori_loop(0, turns + 1, drain, 0)
+
+        @pl.when(row > 0)
+        def _():
+            for slot, other in enumerate(other_chips):
+                level_copy(other, slot).wait_send()
+
+            @pl.when(spot == last)
+            def _():
+                for place in range(last):
+                    edge_copy(0, edge_up, place).wait_send()
+
+            @pl.when(spot == 0)
+            def _():
+                for target in range(chips):
+                    down_copy(target).wait_send()
+
+        @pl.when(row < spans - 1)
+        def _():
+            for slot, other in enumerate(other_chips):
+                end_copy(other, slot).wait_send()
+
+            @pl.when(spot == 0)
+            def _():
+                for place in range(1, span):
+                    edge_copy(1, edge_down, place).wait_send()
+
+        @pl.when(spot > 0)
+        def _():
+            sweep_copy.wait_send()
 
         band_copy.wait_send()
 
@@ -313,18 +631,38 @@
             collective_id=0, has_side_effects=True, vmem_limit_bytes=VMEM_LIMIT
         ),
     )(basis_flux, owner_cell, clogged, conductance, live_count, coupling, leakage)
+    span, depth = planes // 4, 16
+    width = order // chips
+    turns = width // depth
+    row = (1, order)
+    piece = (1, width)
     return pl.pallas_call(
-        functools.partial(chain_kernel, planes, rows, order),
+        functools.partial(chain_kernel, planes, span, chips, rows, order, depth),
         out_shape=jax.ShapeDtypeStruct((1, rows), F32),
         in_specs=[vmem] * 5,
         out_specs=vmem,
         scratch_shapes=[
-            pltpu.VMEM((1, order), F32),
-            pltpu.VMEM((2, 1, order), F32),
-            pltpu.VMEM((2, 1, order), F32),
-            pltpu.VMEM((1, order), F32),
+            pltpu.VMEM((width + depth, order), F32),
+            pltpu.VMEM((width + depth, order), F32),
+            pltpu.VMEM((width, order), F32),
+            pltpu.VMEM((width, order), F32),
+            pltpu.VMEM((width, order), F32),
+            *[pltpu.VMEM((width, order), BF16) for _ in range(6)],
+            pltpu.VMEM(row, F32),
+            pltpu.VMEM((chips, *piece), F32),
+            pltpu.VMEM(row, F32),
+            pltpu.VMEM((chips, *row), F32),
+            *[pltpu.VMEM((chips, *piece), F32) for _ in range(4)],
+            pltpu.VMEM(piece, F32),
+            pltpu.VMEM(piece, F32),
+            pltpu.VMEM(row, F32),
+            pltpu.VMEM(row, F32),
             pltpu.VMEM((1, rows), F32),
-            dma((2,)), dma((2,)), dma, dma,
+            pltpu.VMEM((1, rows), F32),
+            dma((turns + 1,)), dma((turns + 1,)), dma((turns,)), dma((turns,)),
+            dma((chips,)), dma((chips,)), dma((chips,)), dma((chips,)),
+            dma((2, span)), dma((2,)), dma((chips,)), dma((chips,)), dma, dma,
+            dma((chips,)), dma((chips,)), dma, dma,
         ],
         compiler_params=pltpu.CompilerParams(
             collective_id=1, has_side_effects=True, vmem_limit_bytes=VMEM_LIMIT

time: 373 us -> 185 us (0.50)
  Pallas kernels: 371 us -> 183 us
    pallas_call x1, Pallas kernels: 328 us -> 140 us  [per_device(): pl.pallas_call(functools.partial(chain_kernel, planes, span, chips, rows,...]
where the time goes in v2:
time: 185 us
  Pallas kernels  183 us (99%)
    pallas_call x1, Pallas kernels, per_device(): pl.pallas_call(functools.partial(chain_kernel, planes, span, chips, rows,...  140 us
    pallas_call x1, Pallas kernels, per_device(): pl.pallas_call(functools.partial(setup_kernel, planes, chips, rows, order...  43 us

profile of v2, /device:TPU:1, one launch (start us, length us, event | category | flops | bytes accessed | tf_op | source)
XLA Modules:
  0.0 184.5 jit_solution(13679090039544955499)
XLA Ops:
  0.7 43.0 %shard_map.82 = (bf16[1024,1024]{1,0:T(8,128)(2,1)}, bf16[1024,1024]{1,0:T(8,128)(2,1)}, f32[1,1024]{1,0:T(1,128)}) custom-call(bf16[1,128,1024]{2,1,0:T(8,128)(2,1)} %basis.1, s32[1,128]{1,0:T(1,128)} %owner.1, s32[1,128]{1,0:T(1,128)} %clogged.1, f32[1,128]{1,0:T(1,128)} %conductance.1, s32[1,1]{1,0:T(1,128)S(6)} %copy.10.live, f32[1,1024]{1,0:T(1,128)} %coupling.3, ...), custom_call_target="tpu_custom_call" | custom-call | tf_op jit(solution)/shard_map/pallas_call | solution.py:612
  43.6 139.7 %shard_map.83 = f32[1,128]{1,0:T(1,128)} custom-call(bf16[1024,1024]{1,0:T(8,128)(2,1)} %get-tuple-element.8.near_high, bf16[1024,1024]{1,0:T(8,128)(2,1)} %get-tuple-element.9.near_low, f32[1,1024]{1,0:T(1,128)} %get-tuple-element.10.inverse_diag, f32[1,1024]{1,0:T(1,128)} %coupling.3, f32[1,1024]{1,0:T(1,128)} %source.1), custom_call_target="tpu_custom_call" | custom-call | tf_op jit(solution)/shard_map/pallas_call | solution.py:639
  183.3 1.2 copy.11

commit v3 on v2

--- a/solution.py
+++ b/solution.py
@@ -22,38 +22,66 @@
     return high, (value - high.astype(F32)).astype(BF16)
 
 
-def neighbours(plane, planes):
-    return jnp.where(plane > 0, 1, 0) + jnp.where(plane < planes - 1, 1, 0)
-
-
-def setup_kernel(
-    planes, chips, rows, order,
-    basis, owner, clogged, conductance, live, coupling, leakage,
+def kernel(
+    planes, span, chips, rows, order, depth,
+    basis, owner, clogged, conductance, live, coupling, leakage, source,
+    pressure,
     near_high, near_low, inverse_diag,
     slabs, packs, picked, block, gain_high, gain_low, square, faces, faces_in, flux_diag,
+    panel_in, panel_out, back_in, back_out, back_held, low_in, low_out, low_held,
+    panel_high, panel_low, last_high, last_low, back_high, back_low, low_high, low_low,
+    level, parts_out, level_out, level_in, up_pieces, down_pieces, end_pieces, end_out,
+    edge_up, edge_down, edge_mid, total, swept_in, swept, band_out, band_in,
     slab_send, slab_recv, pack_send, pack_recv, face_send, face_recv,
+    panel_send, panel_recv, held_send, held_recv, low_send, low_recv, lowheld_send, lowheld_recv,
+    up_send, up_recv, down_send, down_recv,
+    edge_send, edge_recv, level_send, level_recv, sweep_send, sweep_recv,
+    end_send, end_recv, band_send, band_recv,
 ):
     plane = lax.axis_index("flow")
     me = lax.axis_index("trans")
     parts = 2 * chips
     chip, core = me // 2, lax.rem(me, 2)
-    partner = chip * 2 + 1 - core
+    partner = me + 1 - 2 * core
+    spans = planes // span
+    row, spot = plane // span, lax.rem(plane, span)
+    row_start = row * span
+    last = span - 1
+    width = order // chips
+    turns = width // depth
+    middle = span // 2
+    up_turns = jnp.where(row > 0, turns + 1, 1)
+    down_turns = jnp.where(row < spans - 1, turns, 0)
+    first_column = pl.multiple_of(chip * width, width)
+    face = coupling[...]
+    other_chips = [lax.rem(chip + turn, chips) for turn in range(1, chips)]
     step_rows = 256
     steps = order // step_rows
 
     barrier = pltpu.get_barrier_semaphore()
+
+    def greet(target_plane, target):
+        pl.semaphore_signal(barrier, inc=1, device_id=(target_plane, target), device_id_type=MESH)
+
+    at_end = jnp.logical_or(spot == 0, spot == last)
     for turn in range(1, parts):
-        pl.semaphore_signal(
-            barrier, inc=1, device_id=(plane, lax.rem(me + turn, parts)), device_id_type=MESH
-        )
+        greet(plane, lax.rem(me + turn, parts))
 
     @pl.when(plane > 0)
     def _():
-        pl.semaphore_signal(barrier, inc=1, device_id=(plane - 1, me), device_id_type=MESH)
+        greet(plane - 1, me)
 
     @pl.when(plane < planes - 1)
     def _():
-        pl.semaphore_signal(barrier, inc=1, device_id=(plane + 1, me), device_id_type=MESH)
+        greet(plane + 1, me)
+
+    @pl.when(core == 1)
+    def _():
+        for step, there in ((span, row < spans - 1), (-span, row > 0)):
+            @pl.when(jnp.logical_and(at_end, there))
+            def _():
+                for other in range(chips):
+                    greet(plane + step, other * 2 + 1)
 
     def slab(index):
         return slabs.at[:, pl.ds(pl.multiple_of(index * rows, rows), rows)]
@@ -68,7 +96,10 @@
     packs[me] = jnp.where(row_id == 0, weight, owner[...].astype(F32))
     slabs[:, pl.ds(pl.multiple_of(me * rows, rows), rows)] = basis[0].astype(F32).T.astype(BF16)
 
-    pl.semaphore_wait(barrier, parts - 1 + neighbours(plane, planes))
+    next_to = jnp.where(plane > 0, 1, 0) + jnp.where(plane < planes - 1, 1, 0)
+    across = jnp.where(row > 0, chips, 0) + jnp.where(row < spans - 1, chips, 0)
+    extra = jnp.where(at_end, across, 0)
+    pl.semaphore_wait(barrier, parts - 1 + next_to + jnp.where(core == 1, extra, 0))
 
     def slab_copy(index, target, slot):
         return pltpu.make_async_remote_copy(
@@ -85,10 +116,13 @@
     others = [lax.rem(me + turn, parts) for turn in range(1, parts)]
     for slot, target in enumerate(others):
         pack_copy(me, target, slot).start()
-    away = [lax.rem(chip + turn, chips) * 2 + core for turn in (1, chips - 1, *range(2, chips - 1))]
-    for slot, target in enumerate(away):
-        slab_copy(me, target, slot).start()
-    slab_copy(me, partner, chips - 1).start()
+    way = 1 - 2 * core
+    ahead = lax.rem(chip + way + chips, chips) * 2 + core
+    behind = lax.rem(chip - way + chips, chips) * 2 + core
+    across_ring = lax.rem(chip + 2, chips) * 2 + core
+    slab_copy(me, ahead, 0).start()
+    slab_copy(me, behind, 1).start()
+    slab_copy(me, partner, 2).start()
 
     column = lax.broadcasted_iota(jnp.int32, (rows, order), 1).astype(F32)
 
@@ -99,16 +133,21 @@
         ).astype(BF16)
         return carry
 
-    for source in others:
-        pack_copy(source, partner, 0).wait_recv()
+    for other in others:
+        pack_copy(other, partner, 0).wait_recv()
     lax.fori_loop(0, parts, pick, 0)
 
-    for slot, source in enumerate(away):
-        slab_copy(source, partner, 0).wait_recv()
-        slab_copy(source, partner, chips + slot).start()
+    slab_copy(behind, partner, 0).wait_recv()
+    slab_copy(behind, ahead, 3).start()
+    slab_copy(behind, partner, 4).start()
+    slab_copy(ahead, partner, 0).wait_recv()
+    slab_copy(ahead, partner, 5).start()
+    slab_copy(across_ring, partner, 0).wait_recv()
+    slab_copy(across_ring, partner, 6).start()
     slab_copy(partner, partner, 0).wait_recv()
-    for source in away:
-        slab_copy(source + 1 - 2 * core, partner, 0).wait_recv()
+    flip = 1 - 2 * core
+    for source_slab in (behind, ahead, across_ring):
+        slab_copy(source_slab + flip, partner, 0).wait_recv()
 
     eye = lax.broadcasted_iota(jnp.int32, (rows, rows), 0) == lax.broadcasted_iota(
         jnp.int32, (rows, rows), 1
@@ -119,7 +158,6 @@
             jnp.where(eye, dot(slabs[here, :], picked[:, here]), 0.0), axis=0, keepdims=True
         )
 
-    face = coupling[...]
     leak = leakage[...]
     schur = face * face / (face + leak + flux_diag[...])
     faces[0:1, :] = face
@@ -185,42 +223,17 @@
 
     for slot, target in enumerate(others):
         pack_copy(me, target, slot).wait_send()
-    for slot, target in enumerate(away):
-        slab_copy(me, target, slot).wait_send()
-        slab_copy(target, partner, chips + slot).wait_send()
-    slab_copy(me, partner, chips - 1).wait_send()
+    slab_copy(me, ahead, 0).wait_send()
+    slab_copy(me, behind, 1).wait_send()
+    slab_copy(me, partner, 2).wait_send()
+    slab_copy(behind, ahead, 3).wait_send()
+    slab_copy(behind, partner, 4).wait_send()
+    slab_copy(ahead, partner, 5).wait_send()
+    slab_copy(across_ring, partner, 6).wait_send()
 
     @pl.when(plane < planes - 1)
     def _():
         face_copy(plane + 1).wait_send()
-
-
-def chain_kernel(
-    planes, span, chips, rows, order, depth,
-    near_high, near_low, inverse_diag, coupling, source,
-    pressure,
-    panel_in, panel_out, back_in, back_out, back_held,
-    panel_high, panel_low, last_high, last_low, back_high, back_low,
-    level, parts_out, level_out, level_in, up_pieces, down_pieces, end_pieces, end_out,
-    edge_up, edge_down, swept_in, swept, band_out, band_in,
-    panel_send, panel_recv, held_send, held_recv, up_send, up_recv, down_send, down_recv,
-    edge_send, edge_recv, level_send, level_recv, sweep_send, sweep_recv,
-    end_send, end_recv, band_send, band_recv,
-):
-    plane = lax.axis_index("flow")
-    me = lax.axis_index("trans")
-    chip, core = me // 2, lax.rem(me, 2)
-    partner = me + 1 - 2 * core
-    spans = planes // span
-    row, spot = plane // span, lax.rem(plane, span)
-    row_start = row * span
-    last = span - 1
-    width = order // chips
-    turns = width // depth
-    wide = width // rows
-    first_column = pl.multiple_of(chip * width, width)
-    face = coupling[...]
-    other_chips = [lax.rem(chip + turn, chips) for turn in range(1, chips)]
 
     def remote(source_ref, target_ref, send, recv, target_plane, target):
         return pltpu.make_async_remote_copy(
@@ -256,55 +269,6 @@
     def take(index):
         return pl.ds(pl.multiple_of(index * depth, depth), depth)
 
-    barrier = pltpu.get_barrier_semaphore()
-
-    def greet(target_plane, target):
-        pl.semaphore_signal(barrier, inc=1, device_id=(target_plane, target), device_id_type=MESH)
-
-    greet(plane, partner)
-    inner = jnp.where(spot > 0, 1, 0) + jnp.where(spot < last, 1, 0)
-
-    @pl.when(core == 0)
-    def _():
-        @pl.when(spot > 0)
-        def _():
-            greet(plane - 1, me)
-
-        @pl.when(spot < last)
-        def _():
-            greet(plane + 1, me)
-
-        pl.semaphore_wait(barrier, 1 + inner)
-
-    at_end = jnp.logical_or(spot == 0, spot == last)
-
-    @pl.when(core == 1)
-    def _():
-        for other in other_chips:
-            greet(plane, other * 2 + 1)
-
-        for place in range(span):
-            if place in (0, last):
-                meets = spot != place
-            else:
-                meets = jnp.logical_or(at_end, jnp.abs(spot - place) == 1)
-                meets = jnp.logical_and(meets, spot != place)
-
-            @pl.when(meets)
-            def _():
-                greet(row_start + place, me)
-
-        for step, there in ((span, row < spans - 1), (-span, row > 0)):
-            @pl.when(jnp.logical_and(at_end, there))
-            def _():
-                for other in range(chips):
-                    greet(plane + step, other * 2 + 1)
-
-        beside = jnp.logical_or(spot == 1, spot == last - 1)
-        along = jnp.where(at_end, last, jnp.where(beside, 3, 4))
-        across = jnp.where(row > 0, chips, 0) + jnp.where(row < spans - 1, chips, 0)
-        pl.semaphore_wait(barrier, chips + along + jnp.where(at_end, across, 0))
-
     one_hot_row = lax.broadcasted_iota(jnp.int32, (depth, order), 0)
     one_hot_column = lax.broadcasted_iota(jnp.int32, (depth, order), 1)
 
@@ -327,37 +291,65 @@
 
     band_copy = remote(band_out, band_in, band_send, band_recv, plane, partner)
 
+    def low_copy(index):
+        return remote(
+            low_out.at[take(index), :], low_in.at[take(index), :],
+            low_send.at[index], low_recv.at[index], plane - 1, me,
+        )
+
+    def lowheld_copy(index):
+        return remote(
+            low_out.at[take(index), :], low_held.at[take(index), :],
+            lowheld_send.at[index], lowheld_recv.at[index], plane, partner,
+        )
+
     @pl.when(core == 0)
     def _():
-        def flow(index, carry):
-            @pl.when(spot == last)
-            def _():
-                back_in[take(index), :] = unit_rows(index)
-
-            @pl.when(spot < last)
-            def _():
-                back_copy(index).wait_recv()
-
-            back_out[take(index), :] = apply(face * back_in[take(index), :])
-
-            @pl.when(spot > 0)
-            def _():
-                back_copy(index).start()
-
-            held_copy(index).start()
-            return carry
-
-        lax.fori_loop(0, turns, flow, 0)
-
-        def drain(index, carry):
-            @pl.when(spot > 0)
-            def _():
-                back_copy(index).wait_send()
-
-            held_copy(index).wait_send()
-            return carry
-
-        lax.fori_loop(0, turns, drain, 0)
+        def flow_down(top, came, went, pass_on, keep):
+            def flow(index, carry):
+                @pl.when(spot == top)
+                def _():
+                    came[take(index), :] = unit_rows(index)
+
+                @pl.when(spot < top)
+                def _():
+                    pass_on(index).wait_recv()
+
+                went[take(index), :] = apply(face * came[take(index), :])
+
+                @pl.when(spot > 0)
+                def _():
+                    pass_on(index).start()
+
+                keep(index).start()
+                return carry
+
+            return flow
+
+        def drain(pass_on, keep):
+            def wait(index, carry):
+                @pl.when(spot > 0)
+                def _():
+                    pass_on(index).wait_send()
+
+                keep(index).wait_send()
+                return carry
+
+            return wait
+
+        @pl.when(spot < middle)
+        def _():
+            lax.fori_loop(
+                0, turns, flow_down(middle - 1, low_in, low_out, low_copy, lowheld_copy), 0
+            )
+
+        lax.fori_loop(0, down_turns, flow_down(last, back_in, back_out, back_copy, held_copy), 0)
+
+        @pl.when(spot < middle)
+        def _():
+            lax.fori_loop(0, turns, drain(low_copy, lowheld_copy), 0)
+
+        lax.fori_loop(0, down_turns, drain(back_copy, held_copy), 0)
         band_copy.wait_recv()
         pressure[...] = band_in[...]
 
@@ -425,22 +417,29 @@
                     one_hot_row == 0, source[...], 0.0
                 )
 
-            panel_out[take(index), :] = face * apply(panel_in[take(index), :])
+            arrived_rows = panel_in[take(index), :]
+            moved = face * apply(arrived_rows)
+            panel_out[take(index), :] = moved
 
             @pl.when(spot < last)
             def _():
                 panel_copy(index).start()
 
+            @pl.when(turn > 0)
+            def _():
+                panel_high[take(index), :], panel_low[take(index), :] = split(arrived_rows)
+
+                @pl.when(spot == last)
+                def _():
+                    last_high[take(index), :], last_low[take(index), :] = split(moved)
+
             return carry
 
-        lax.fori_loop(0, turns + 1, flow, 0)
-        panel_high[...], panel_low[...] = split(panel_in[0:width, :])
+        lax.fori_loop(0, up_turns, flow, 0)
         level[...] = panel_in[width : width + 1, :]
 
         @pl.when(spot == last)
         def _():
-            last_high[...], last_low[...] = split(panel_out[0:width, :])
-
             @pl.when(row > 0)
             def _():
                 for target in range(chips):
@@ -454,9 +453,16 @@
             def _():
                 edge_up[...] = jnp.zeros_like(edge_up)
 
+            @pl.when(row == 0)
+            def _():
+                parts_out[...] = jnp.zeros_like(parts_out)
+
+            @pl.when(jnp.logical_and(row > 0, row < spans - 1))
+            def _():
+                cut(by_panel(edge_up[...], last_high, last_low), parts_out)
+
             @pl.when(row < spans - 1)
             def _():
-                cut(by_panel(edge_up[...], last_high, last_low), parts_out)
                 parts_out[chip] = parts_out[chip] + panel_out[
                     width : width + 1, pl.ds(first_column, width)
                 ]
@@ -485,32 +491,52 @@
                 ).wait_recv()
             level[...] = level[...] + ((level_in[0] + level_in[1]) + (level_in[2] + level_in[3]))
 
-        @pl.when(spot < last)
+        @pl.when(jnp.logical_and(spot != last, spot != middle - 1))
         def _():
             sweep_copy.wait_recv()
             level[...] = level[...] + face * swept_in[...]
 
         swept[...] = apply_one(level[...])
 
-        @pl.when(spot > 0)
+        @pl.when(jnp.logical_and(spot != 0, spot != middle))
         def _():
             sweep_copy.start()
 
-        def arrived(index, carry):
-            held_copy(index).wait_recv()
-            return carry
-
-        lax.fori_loop(0, turns, arrived, 0)
-        back_high[...], back_low[...] = split(back_held[...])
+        @pl.when(spot == middle)
+        def _():
+            edge_mid[...] = swept[:, pl.ds(first_column, width)]
+            for place in (0, *range(middle - 1, 0, -1)):
+                edge_copy(2, edge_mid, place).start()
+
+        def arrived(keep):
+            def wait(index, carry):
+                keep(index).wait_recv()
+                return carry
+
+            return wait
+
+        total[...] = jnp.zeros_like(total)
+
+        @pl.when(row < spans - 1)
+        def _():
+            lax.fori_loop(0, turns, arrived(held_copy), 0)
+            back_high[...], back_low[...] = split(back_held[...])
+
+        @pl.when(spot < middle)
+        def _():
+            lax.fori_loop(0, turns, arrived(lowheld_copy), 0)
+            low_high[...], low_low[...] = split(low_held[...])
+            edge_copy(2, edge_mid, 0).wait_recv()
+            total[...] = by_panel(edge_mid[...], low_high, low_low)
 
         @pl.when(jnp.logical_and(spot == last, row < spans - 1))
         def _():
             for target in range(chips):
                 up_copy(target).wait_send()
 
-        @pl.when(spot == 0)
-        def _():
-            @pl.when(row < spans - 1)
+        @pl.when(row < spans - 1)
+        def _():
+            @pl.when(spot == 0)
             def _():
                 for target in range(chips):
                     remote(
@@ -521,13 +547,17 @@
                     down_pieces[2] + down_pieces[3]
                 )
 
-            @pl.when(row == spans - 1)
-            def _():
-                edge_down[...] = jnp.zeros_like(edge_down)
-
+            @pl.when(spot > 0)
+            def _():
+                edge_copy(1, edge_down, 0).wait_recv()
+
+            total[...] = total[...] + by_panel(edge_down[...], back_high, back_low)
+
+        @pl.when(spot == 0)
+        def _():
             @pl.when(row > 0)
             def _():
-                cut(by_panel(edge_down[...], back_high, back_low), parts_out)
+                cut(total[...], parts_out)
                 parts_out[chip] = parts_out[chip] + swept[:, pl.ds(first_column, width)]
                 for target in range(chips):
                     down_copy(target).start()
@@ -538,14 +568,11 @@
                     edge_copy(1, edge_down, place).start()
 
         end_pieces[chip] = jnp.zeros((1, width), F32)
-
-        @pl.when(row < spans - 1)
-        def _():
-            @pl.when(spot > 0)
-            def _():
-                edge_copy(1, edge_down, 0).wait_recv()
-
-            cut(by_panel(edge_down[...], back_high, back_low), end_out)
+        corrected = jnp.logical_or(row < spans - 1, spot < middle)
+
+        @pl.when(corrected)
+        def _():
+            cut(total[...], end_out)
             for slot, other in enumerate(other_chips):
                 end_copy(other, slot).start()
             end_pieces[chip] = end_out[chip]
@@ -563,11 +590,11 @@
 
         @pl.when(spot < last)
         def _():
-            def drain(index, carry):
-                panel_copy(index).wait_send()
+            def drain(turn, carry):
+                panel_copy(lax.rem(turn + turns, turns + 1)).wait_send()
                 return carry
 
-            lax.fori_loop(0, turns + 1, drain, 0)
+            lax.fori_loop(0, up_turns, drain, 0)
 
         @pl.when(row > 0)
         def _():
@@ -584,17 +611,22 @@
                 for target in range(chips):
                     down_copy(target).wait_send()
 
-        @pl.when(row < spans - 1)
+        @pl.when(corrected)
         def _():
             for slot, other in enumerate(other_chips):
                 end_copy(other, slot).wait_send()
 
-            @pl.when(spot == 0)
-            def _():
-                for place in range(1, span):
-                    edge_copy(1, edge_down, place).wait_send()
-
-        @pl.when(spot > 0)
+        @pl.when(jnp.logical_and(row < spans - 1, spot == 0))
+        def _():
+            for place in range(1, span):
+                edge_copy(1, edge_down, place).wait_send()
+
+        @pl.when(spot == middle)
+        def _():
+            for place in range(middle):
+                edge_copy(2, edge_mid, place).wait_send()
+
+        @pl.when(jnp.logical_and(spot != 0, spot != middle))
         def _():
             sweep_copy.wait_send()
 
@@ -606,48 +638,33 @@
     parts = lax.axis_size("trans")
     chips = parts // 2
     rows, order = basis_flux.shape[1:]
-    vmem = pl.BlockSpec(memory_space=pltpu.VMEM)
-    dma = pltpu.SemaphoreType.DMA
-    matrix = jax.ShapeDtypeStruct((order, order), BF16)
-    near_high, near_low, inverse_diag = pl.pallas_call(
-        functools.partial(setup_kernel, planes, chips, rows, order),
-        out_shape=(matrix, matrix, jax.ShapeDtypeStruct((1, order), F32)),
-        in_specs=[vmem] * 7,
-        out_specs=(vmem,) * 3,
-        scratch_shapes=[
-            pltpu.VMEM((order, parts * rows), BF16),
-            pltpu.VMEM((parts, 8, rows), F32),
-            pltpu.VMEM((parts * rows, order), BF16),
-            pltpu.VMEM((order, order), F32),
-            pltpu.VMEM((order, order), BF16),
-            pltpu.VMEM((order, order), BF16),
-            pltpu.VMEM((order, order), BF16),
-            pltpu.VMEM((2, order), F32),
-            pltpu.VMEM((2, order), F32),
-            pltpu.VMEM((1, order), F32),
-            dma((parts,)), dma((parts,)), dma((parts,)), dma((parts,)), dma, dma,
-        ],
-        compiler_params=pltpu.CompilerParams(
-            collective_id=0, has_side_effects=True, vmem_limit_bytes=VMEM_LIMIT
-        ),
-    )(basis_flux, owner_cell, clogged, conductance, live_count, coupling, leakage)
     span, depth = planes // 4, 16
     width = order // chips
     turns = width // depth
     row = (1, order)
     piece = (1, width)
+    vmem = pl.BlockSpec(memory_space=pltpu.VMEM)
+    dma = pltpu.SemaphoreType.DMA
+    half = pltpu.VMEM((order, order), BF16)
     return pl.pallas_call(
-        functools.partial(chain_kernel, planes, span, chips, rows, order, depth),
+        functools.partial(kernel, planes, span, chips, rows, order, depth),
         out_shape=jax.ShapeDtypeStruct((1, rows), F32),
-        in_specs=[vmem] * 5,
+        in_specs=[vmem] * 8,
         out_specs=vmem,
         scratch_shapes=[
+            half, half, pltpu.VMEM(row, F32),
+            half,
+            pltpu.VMEM((parts, 8, rows), F32),
+            half,
+            pltpu.VMEM((order, order), F32),
+            half, half, half,
+            pltpu.VMEM((2, order), F32),
+            pltpu.VMEM((2, order), F32),
+            pltpu.VMEM(row, F32),
             pltpu.VMEM((width + depth, order), F32),
             pltpu.VMEM((width + depth, order), F32),
-            pltpu.VMEM((width, order), F32),
-            pltpu.VMEM((width, order), F32),
-            pltpu.VMEM((width, order), F32),
-            *[pltpu.VMEM((width, order), BF16) for _ in range(6)],
+            *[pltpu.VMEM((width, order), F32) for _ in range(6)],
+            *[pltpu.VMEM((width, order), BF16) for _ in range(8)],
             pltpu.VMEM(row, F32),
             pltpu.VMEM((chips, *piece), F32),
             pltpu.VMEM(row, F32),
@@ -655,19 +672,23 @@
             *[pltpu.VMEM((chips, *piece), F32) for _ in range(4)],
             pltpu.VMEM(piece, F32),
             pltpu.VMEM(piece, F32),
+            pltpu.VMEM(piece, F32),
+            pltpu.VMEM(row, F32),
             pltpu.VMEM(row, F32),
             pltpu.VMEM(row, F32),
             pltpu.VMEM((1, rows), F32),
             pltpu.VMEM((1, rows), F32),
+            dma((parts,)), dma((parts,)), dma((parts,)), dma((parts,)), dma, dma,
             dma((turns + 1,)), dma((turns + 1,)), dma((turns,)), dma((turns,)),
+            dma((turns,)), dma((turns,)), dma((turns,)), dma((turns,)),
             dma((chips,)), dma((chips,)), dma((chips,)), dma((chips,)),
-            dma((2, span)), dma((2,)), dma((chips,)), dma((chips,)), dma, dma,
+            dma((3, span)), dma((3,)), dma((chips,)), dma((chips,)), dma, dma,
             dma((chips,)), dma((chips,)), dma, dma,
         ],
         compiler_params=pltpu.CompilerParams(
-            collective_id=1, has_side_effects=True, vmem_limit_bytes=VMEM_LIMIT
+            collective_id=0, has_side_effects=True, vmem_limit_bytes=VMEM_LIMIT
         ),
-    )(near_high, near_low, inverse_diag, coupling, source)
+    )(basis_flux, owner_cell, clogged, conductance, live_count, coupling, leakage, source)
 
 
 def solution(mesh):

time: 185 us -> 158 us (0.85)
  Pallas kernels: 183 us -> 156 us
    pallas_call x2 -> x1, Pallas kernels: 183 us -> 156 us  [per_device(): pl.pallas_call(functools.partial(kernel, planes, span, chips, rows, order...]
where the time goes in v3:
time: 158 us
  Pallas kernels  156 us (99%)
    pallas_call x1, Pallas kernels, per_device(): pl.pallas_call(functools.partial(kernel, planes, span, chips, rows, order...  156 us

profile of v3, /device:TPU:1, one launch (start us, length us, event | category | flops | bytes accessed | tf_op | source)
XLA Modules:
  0.0 158.2 jit_solution(16732927991087083914)
XLA Ops:
  0.7 156.3 %shard_map.82 = f32[1,128]{1,0:T(1,128)} custom-call(bf16[1,128,1024]{2,1,0:T(8,128)(2,1)} %basis.1, s32[1,128]{1,0:T(1,128)} %owner.1, s32[1,128]{1,0:T(1,128)} %clogged.1, f32[1,128]{1,0:T(1,128)} %conductance.1, s32[1,1]{1,0:T(1,128)S(6)} %copy.10.live, f32[1,1024]{1,0:T(1,128)} %coupling.1, f32[1,1024]{1,0:T(1,128)} %leakage.1, f32[1,1024]{1,0:T(1,128)} %source.1), custom_call_target="tpu_custom_call" | custom-call | tf_op jit(solution)/shard_map/pallas_call | solution.py:649
  157.0 1.2 copy.11

commit v4 on v3

v4 whole, which is shorter than its diff:
```python
import functools

import jax
import jax.numpy as jnp
from jax import lax
from jax.experimental import pallas as pl
from jax.experimental.pallas import tpu as pltpu
from jax.sharding import PartitionSpec as P

MESH = pl.DeviceIdType.MESH
BF16 = jnp.bfloat16
F32 = jnp.float32
VMEM_LIMIT = 56 * 1024 * 1024


def dot(left, right):
    return jnp.dot(left, right, preferred_element_type=F32)


def split(value):
    high = value.astype(BF16)
    return high, (value - high.astype(F32)).astype(BF16)


def kernel(
    planes, span, chips, rows, order, depth, tops,
    basis, owner, clogged, conductance, live, coupling, leakage, source,
    pressure,
    near_high, near_low, inverse_diag,
    slabs, packs, picked, block, gain_high, gain_low, square, faces, faces_in, flux_diag,
    panel_in, panel_out, back_in, back_out, back_high, back_low,
    panel_high, panel_low, last_high, last_low,
    level, parts_out, up_pieces, down_pieces, edge_pieces, end_pieces, end_out,
    edge_up, edges, total, swept_in, swept, system_diag,
    slab_send, slab_recv, pack_send, pack_recv, face_send, face_recv,
    panel_send, panel_recv, back_send, back_recv, held_send, held_recv,
    up_send, up_recv, down_send, down_recv,
    edge_send, edge_recv, mid_send, mid_recv, sweep_send, sweep_recv, end_send, end_recv,
):
    plane = lax.axis_index("flow")
    me = lax.axis_index("trans")
    parts = 2 * chips
    chip, core = me // 2, lax.rem(me, 2)
    partner = me + 1 - 2 * core
    spans = planes // span
    row, spot = plane // span, lax.rem(plane, span)
    row_start = row * span
    last = span - 1
    width = order // chips
    turns = width // depth
    bottoms = tuple(top + 1 for top in tops[1:]) + (0,)
    up_turns = jnp.where(row > 0, turns + 1, 1)

    def one_of(places):
        return functools.reduce(jnp.logical_or, [spot == place for place in places])

    first_column = pl.multiple_of(chip * width, width)
    face = coupling[...]
    other_chips = [lax.rem(chip + turn, chips) for turn in range(1, chips)]
    step_rows = 256
    steps = order // step_rows

    barrier = pltpu.get_barrier_semaphore()

    def greet(target_plane, target):
        pl.semaphore_signal(barrier, inc=1, device_id=(target_plane, target), device_id_type=MESH)

    for turn in range(1, parts):
        greet(plane, lax.rem(me + turn, parts))

    @pl.when(plane > 0)
    def _():
        greet(plane - 1, me)

    @pl.when(plane < planes - 1)
    def _():
        greet(plane + 1, me)

    @pl.when(jnp.logical_and(core == 1, jnp.logical_and(row > 0, one_of(tops))))
    def _():
        for other in range(chips):
            greet(row_start - 1, other * 2 + 1)

    def slab(index):
        return slabs.at[:, pl.ds(pl.multiple_of(index * rows, rows), rows)]

    position = lax.broadcasted_iota(jnp.int32, (1, rows), 1)
    weight = (
        conductance[...]
        * (1 - clogged[...]).astype(F32)
        * (position < live[...]).astype(F32)
    ).astype(BF16).astype(F32)
    row_id = lax.broadcasted_iota(jnp.int32, (8, rows), 0)
    packs[me] = jnp.where(row_id == 0, weight, owner[...].astype(F32))
    slabs[:, pl.ds(pl.multiple_of(me * rows, rows), rows)] = basis[0].astype(F32).T.astype(BF16)

    next_to = jnp.where(plane > 0, 1, 0) + jnp.where(plane < planes - 1, 1, 0)
    sends_up = jnp.logical_and(core == 1, jnp.logical_and(spot == last, row < spans - 1))
    extra = jnp.where(sends_up, chips * len(tops), 0)
    pl.semaphore_wait(barrier, parts - 1 + next_to + extra)

    def slab_copy(index, target, slot):
        return pltpu.make_async_remote_copy(
            slab(index), slab(index), slab_send.at[slot], slab_recv.at[index],
            device_id=(plane, target), device_id_type=MESH,
        )

    def pack_copy(index, target, slot):
        return pltpu.make_async_remote_copy(
            packs.at[index], packs.at[index], pack_send.at[slot], pack_recv.at[index],
            device_id=(plane, target), device_id_type=MESH,
        )

    others = [lax.rem(me + turn, parts) for turn in range(1, parts)]
    for slot, target in enumerate(others):
        pack_copy(me, target, slot).start()
    way = 1 - 2 * core
    ahead = lax.rem(chip + way + chips, chips) * 2 + core
    behind = lax.rem(chip - way + chips, chips) * 2 + core
    across_ring = lax.rem(chip + 2, chips) * 2 + core
    slab_copy(me, ahead, 0).start()
    slab_copy(me, behind, 1).start()
    slab_copy(me, partner, 2).start()

    column = lax.broadcasted_iota(jnp.int32, (rows, order), 1).astype(F32)

    def pick(index, carry):
        turned = packs[index].T
        picked[pl.ds(pl.multiple_of(index * rows, rows), rows), :] = jnp.where(
            turned[:, 1:2] == column, turned[:, 0:1], 0.0
        ).astype(BF16)
        return carry

    for other in others:
        pack_copy(other, partner, 0).wait_recv()
    lax.fori_loop(0, parts, pick, 0)

    slab_copy(behind, partner, 0).wait_recv()
    slab_copy(behind, ahead, 3).start()
    slab_copy(behind, partner, 4).start()
    slab_copy(ahead, partner, 0).wait_recv()
    slab_copy(ahead, partner, 5).start()
    slab_copy(across_ring, partner, 0).wait_recv()
    slab_copy(across_ring, partner, 6).start()
    slab_copy(partner, partner, 0).wait_recv()
    flip = 1 - 2 * core
    for source_slab in (behind, ahead, across_ring):
        slab_copy(source_slab + flip, partner, 0).wait_recv()

    eye = lax.broadcasted_iota(jnp.int32, (rows, rows), 0) == lax.broadcasted_iota(
        jnp.int32, (rows, rows), 1
    )
    for index in range(order // rows):
        here = pl.ds(index * rows, rows)
        flux_diag[:, here] = jnp.sum(
            jnp.where(eye, dot(slabs[here, :], picked[:, here]), 0.0), axis=0, keepdims=True
        )

    leak = leakage[...]
    schur = face * face / (face + leak + flux_diag[...])
    faces[0:1, :] = face
    faces[1:2, :] = schur

    def face_copy(target):
        return pltpu.make_async_remote_copy(
            faces, faces_in, face_send, face_recv, device_id=(target, me), device_id_type=MESH
        )

    @pl.when(plane < planes - 1)
    def _():
        face_copy(plane + 1).start()

    def assemble(index, carry):
        here = pl.ds(pl.multiple_of(index * step_rows, step_rows), step_rows)
        block[here, :] = dot(slabs[here, :], picked[...])
        return carry

    lax.fori_loop(0, steps, assemble, 0)

    @pl.when(plane > 0)
    def _():
        face_copy(plane).wait_recv()

    @pl.when(plane == 0)
    def _():
        faces_in[...] = jnp.zeros_like(faces_in)

    diag = flux_diag[...] + (leak + face + faces_in[0:1, :] - faces_in[1:2, :])
    pivots = 1.0 / diag
    inverse_diag[...] = pivots
    system_diag[...] = diag

    across = lax.broadcasted_iota(jnp.int32, (step_rows, order), 1)
    down = lax.broadcasted_iota(jnp.int32, (step_rows, order), 0)

    def scale(index, carry):
        here = pl.ds(pl.multiple_of(index * step_rows, step_rows), step_rows)
        gain = jnp.where(across == down + index * step_rows, 0.0, block[here, :] * pivots)
        block[here, :] = gain
        gain_high[here, :], gain_low[here, :] = split(gain)
        return carry

    lax.fori_loop(0, steps, scale, 0)

    def squared(index, carry):
        here = pl.ds(pl.multiple_of(index * step_rows, step_rows), step_rows)
        high, low = gain_high[here, :], gain_low[here, :]
        value = dot(high, gain_high[...]) + (dot(high, gain_low[...]) + dot(low, gain_high[...]))
        square[here, :] = value.astype(BF16)
        block[here, :] = value - block[here, :]
        return carry

    lax.fori_loop(0, steps, squared, 0)

    def finish(index, carry):
        here = pl.ds(pl.multiple_of(index * step_rows, step_rows), step_rows)
        near = block[here, :] - dot(gain_high[here, :], square[...])
        near_high[here, :], near_low[here, :] = split(near)
        return carry

    lax.fori_loop(0, steps, finish, 0)

    for slot, target in enumerate(others):
        pack_copy(me, target, slot).wait_send()
    slab_copy(me, ahead, 0).wait_send()
    slab_copy(me, behind, 1).wait_send()
    slab_copy(me, partner, 2).wait_send()
    slab_copy(behind, ahead, 3).wait_send()
    slab_copy(behind, partner, 4).wait_send()
    slab_copy(ahead, partner, 5).wait_send()
    slab_copy(across_ring, partner, 6).wait_send()

    @pl.when(plane < planes - 1)
    def _():
        face_copy(plane + 1).wait_send()

    def remote(source_ref, target_ref, send, recv, target_plane, target):
        return pltpu.make_async_remote_copy(
            source_ref, target_ref, send, recv,
            device_id=(target_plane, target), device_id_type=MESH,
        )

    def apply(value):
        count = value.shape[0]
        scaled = value * inverse_diag[...]
        high = scaled.astype(BF16).astype(F32)
        both = jnp.concatenate([high, scaled - high], axis=0).astype(BF16)
        by_high = dot(both, near_high[...])
        by_low = dot(both[:count], near_low[...])
        return scaled + (by_high[:count] + (by_high[count:] + by_low)), both[:count], both[count:]

    def two_rows(value):
        row_id = lax.broadcasted_iota(jnp.int32, (8, value.shape[1]), 0)
        high = value.astype(BF16).astype(F32)
        return jnp.where(row_id == 0, high, jnp.where(row_id == 1, value - high, 0.0)).astype(BF16)

    def apply_one(value):
        scaled = value * inverse_diag[...]
        both = two_rows(scaled)
        return scaled + jnp.sum(
            dot(both, near_high[...]) + dot(both, near_low[...]), axis=0, keepdims=True
        )

    def by_panel(value, high, low):
        both = two_rows(value)
        return jnp.sum(dot(both, high[...]) + dot(both, low[...]), axis=0, keepdims=True)

    def take(index):
        return pl.ds(pl.multiple_of(index * depth, depth), depth)

    one_hot_row = lax.broadcasted_iota(jnp.int32, (depth, order), 0)
    one_hot_column = lax.broadcasted_iota(jnp.int32, (depth, order), 1)

    def unit_rows(index):
        return jnp.where(
            one_hot_column == one_hot_row + (chip * width + index * depth), 1.0, 0.0
        )

    def back_copy(index):
        return remote(
            back_out.at[take(index), :], back_in.at[take(index), :],
            back_send.at[index], back_recv.at[index], plane - 1, me,
        )

    def held_copy(index, half):
        ref = back_low if half else back_high
        return remote(
            ref.at[take(index), :], ref.at[take(index), :],
            held_send.at[half, index], held_recv.at[half, index // turns], plane, partner,
        )

    def stream_turns(stream):
        active = spot <= tops[stream]
        if stream == 0:
            active = jnp.logical_and(active, row < spans - 1)
        return jnp.where(active, turns, 0)

    def end_copy(target):
        return remote(
            end_out.at[target], end_pieces.at[chip], end_send.at[target], end_recv.at[chip],
            plane, target,
        )

    def end_from(source_chip):
        return remote(
            end_out.at[0], end_pieces.at[source_chip], end_send.at[0], end_recv.at[source_chip],
            plane, me,
        )

    @pl.when(core == 0)
    def _():
        def flow_down(stream, top):
            def flow(turn, carry):
                index = stream * turns + turn

                @pl.when(spot == top)
                def _():
                    back_in[take(index), :] = unit_rows(turn)

                @pl.when(spot < top)
                def _():
                    back_copy(index).wait_recv()

                moved = apply(face * back_in[take(index), :])[0]
                back_out[take(index), :] = moved

                @pl.when(spot > 0)
                def _():
                    back_copy(index).start()

                back_high[take(index), :], back_low[take(index), :] = split(moved)
                held_copy(index, 0).start()
                held_copy(index, 1).start()
                return carry

            return flow

        def drain(stream):
            def wait(turn, carry):
                index = stream * turns + turn

                @pl.when(spot > 0)
                def _():
                    back_copy(index).wait_send()

                held_copy(index, 0).wait_send()
                held_copy(index, 1).wait_send()
                return carry

            return wait

        for stream in range(len(tops) - 1, -1, -1):
            lax.fori_loop(0, stream_turns(stream), flow_down(stream, tops[stream]), 0)
        for stream in range(len(tops) - 1, -1, -1):
            lax.fori_loop(0, stream_turns(stream), drain(stream), 0)
        for target in range(chips):
            end_from(target).wait_recv()
        pressure[...] = (end_pieces[0] + end_pieces[1]) + (end_pieces[2] + end_pieces[3])

    def panel_copy(index):
        return remote(
            panel_out.at[take(index), :], panel_in.at[take(index), :],
            panel_send.at[index], panel_recv.at[index], plane + 1, me,
        )

    def up_copy(target, part):
        return remote(
            parts_out.at[target], up_pieces.at[chip],
            up_send.at[part, target], up_recv.at[chip],
            row_start + span + tops[part], target * 2 + 1,
        )

    def down_copy(target, place):
        return remote(
            parts_out.at[target], down_pieces.at[chip],
            down_send.at[place, target], down_recv.at[chip],
            row_start - span + place, target * 2 + 1,
        )

    def edge_copy(place):
        return remote(
            edge_up, edge_up, edge_send.at[place], edge_recv, row_start + place, me
        )

    def mid_copy(stream, target, place):
        return remote(
            parts_out.at[target], edge_pieces.at[stream, chip],
            mid_send.at[place, target], mid_recv.at[stream, chip],
            row_start + place, target * 2 + 1,
        )

    sweep_copy = remote(swept, swept_in, sweep_send, sweep_recv, plane - 1, me)

    def cut(value, ref, count, size):
        for index in range(count):
            ref[index] = value[:, index * size : (index + 1) * size]

    @pl.when(core == 1)
    def _():
        def flow(turn, carry):
            index = lax.rem(turn + turns, turns + 1)

            @pl.when(spot == 0)
            def _():
                panel_in[take(index), :] = unit_rows(index)

            @pl.when(spot > 0)
            def _():
                panel_copy(index).wait_recv()

            @pl.when(turn == 0)
            def _():
                @pl.when(spot == 0)
                def _():
                    panel_in[take(index), :] = jnp.zeros((depth, order), F32)

                panel_in[take(index), :] = panel_in[take(index), :] + jnp.where(
                    one_hot_row == 0, source[...], 0.0
                )

            arrived_rows = panel_in[take(index), :]
            applied, high, low = apply(arrived_rows)
            moved = face * applied
            panel_out[take(index), :] = moved

            @pl.when(spot < last)
            def _():
                panel_copy(index).start()

            @pl.when(turn > 0)
            def _():
                panel_high[take(index), :] = high
                panel_low[take(index), :] = low

                @pl.when(spot == last)
                def _():
                    last_high[take(index), :], last_low[take(index), :] = split(moved)

            return carry

        lax.fori_loop(0, up_turns, flow, 0)
        level[...] = jnp.where(chip == 0, panel_in[width : width + 1, :], 0.0)

        def gather_pieces(pieces, sems):
            for target in range(chips):
                remote(
                    parts_out.at[target], pieces.at[target], end_send.at[0], sems.at[target],
                    plane, me,
                ).wait_recv()
            return (pieces[0] + pieces[1]) + (pieces[2] + pieces[3])

        @pl.when(jnp.logical_and(row > 0, one_of(tops)))
        def _():
            edge_up[...] = gather_pieces(up_pieces, up_recv)

        @pl.when(jnp.logical_and(spot == last, row < spans - 1))
        def _():
            @pl.when(row == 0)
            def _():
                parts_out[...] = jnp.zeros_like(parts_out)

            @pl.when(row > 0)
            def _():
                cut(by_panel(edge_up[...], last_high, last_low), parts_out, chips, width)

            parts_out[chip] = parts_out[chip] + panel_out[
                width : width + 1, pl.ds(first_column, width)
            ]
            for part in range(len(tops)):
                for target in range(chips):
                    up_copy(target, part).start()

        @pl.when(row > 0)
        def _():
            for top, bottom in zip(tops, bottoms):
                @pl.when(spot == top)
                def _():
                    for place in range(top - 1, bottom - 1, -1):
                        edge_copy(place).start()

            @pl.when(jnp.logical_not(one_of(tops)))
            def _():
                edge_copy(0).wait_recv()

            level[...] = level[...] + system_diag[...] * by_panel(
                edge_up[...], panel_high, panel_low
            )

        @pl.when(jnp.logical_not(one_of(tops)))
        def _():
            sweep_copy.wait_recv()
            level[...] = level[...] + face * swept_in[...]

        swept[...] = apply_one(level[...])

        @pl.when(jnp.logical_not(one_of(bottoms)))
        def _():
            sweep_copy.start()

        for stream in range(1, len(tops)):
            @pl.when(spot == bottoms[stream - 1])
            def _():
                cut(swept[...], parts_out, chips, width)

                def send_mid(place, carry):
                    for target in range(chips):
                        mid_copy(stream, target, place).start()
                    return carry

                lax.fori_loop(0, tops[stream] + 1, send_mid, 0)

        def arrived(stream):
            here = pl.ds(stream * width, width)
            for half, ref in enumerate((back_high, back_low)):
                remote(
                    ref.at[here, :], ref.at[here, :],
                    held_send.at[half, 0], held_recv.at[half, stream], plane, me,
                ).wait_recv()

        def by_stream(stream):
            here = slice(stream * width, (stream + 1) * width)
            return by_panel(edges[stream], back_high.at[here, :], back_low.at[here, :])

        total[...] = swept[...]
        for stream in range(len(tops) - 1, -1, -1):
            @pl.when(stream_turns(stream) > 0)
            def _():
                arrived(stream)

        for stream in range(1, len(tops)):
            @pl.when(spot <= tops[stream])
            def _():
                edges[stream] = gather_pieces(edge_pieces.at[stream], mid_recv.at[stream])
                total[...] = total[...] + by_stream(stream)

        @pl.when(row < spans - 1)
        def _():
            edges[0] = gather_pieces(down_pieces, down_recv)
            total[...] = total[...] + by_stream(0)

        @pl.when(jnp.logical_and(spot == 0, row > 0))
        def _():
            cut(total[...], parts_out, chips, width)

            def send_down(place, carry):
                for target in range(chips):
                    down_copy(target, place).start()
                return carry

            lax.fori_loop(0, span, send_down, 0)

        cut(total[...], end_out, parts, rows)
        for target in others:
            end_copy(target).start()
        end_pieces[chip] = end_out[me]
        for other in other_chips:
            end_from(other).wait_recv()
        pressure[...] = (end_pieces[0] + end_pieces[1]) + (end_pieces[2] + end_pieces[3])

        @pl.when(spot < last)
        def _():
            def drain(turn, carry):
                panel_copy(lax.rem(turn + turns, turns + 1)).wait_send()
                return carry

            lax.fori_loop(0, up_turns, drain, 0)

        @pl.when(jnp.logical_and(spot == last, row < spans - 1))
        def _():
            for part in range(len(tops)):
                for target in range(chips):
                    up_copy(target, part).wait_send()

        @pl.when(row > 0)
        def _():
            for top, bottom in zip(tops, bottoms):
                @pl.when(spot == top)
                def _():
                    for place in range(top - 1, bottom - 1, -1):
                        edge_copy(place).wait_send()

        @pl.when(jnp.logical_and(spot == 0, row > 0))
        def _():
            def sent_down(place, carry):
                for target in range(chips):
                    down_copy(target, place).wait_send()
                return carry

            lax.fori_loop(0, span, sent_down, 0)

        for stream in range(1, len(tops)):
            @pl.when(spot == bottoms[stream - 1])
            def _():
                def sent_mid(place, carry):
                    for target in range(chips):
                        mid_copy(stream, target, place).wait_send()
                    return carry

                lax.fori_loop(0, tops[stream] + 1, sent_mid, 0)

        @pl.when(jnp.logical_not(one_of(bottoms)))
        def _():
            sweep_copy.wait_send()

        for target in others:
            end_copy(target).wait_send()


def per_device(basis_flux, owner_cell, clogged, conductance, live_count, coupling, leakage, source):
    planes = lax.axis_size("flow")
    parts = lax.axis_size("trans")
    chips = parts // 2
    rows, order = basis_flux.shape[1:]
    span, depth = planes // 4, 16
    tops = (15, 10, 7, 4)
    streams = len(tops)
    width = order // chips
    turns = width // depth
    row = (1, order)
    piece = (1, width)
    vmem = pl.BlockSpec(memory_space=pltpu.VMEM)
    dma = pltpu.SemaphoreType.DMA
    half = pltpu.VMEM((order, order), BF16)
    return pl.pallas_call(
        functools.partial(kernel, planes, span, chips, rows, order, depth, tops),
        out_shape=jax.ShapeDtypeStruct((1, rows), F32),
        in_specs=[vmem] * 8,
        out_specs=vmem,
        scratch_shapes=[
            half, half, pltpu.VMEM(row, F32),
            half,
            pltpu.VMEM((parts, 8, rows), F32),
            half,
            pltpu.VMEM((order, order), F32),
            half, half, half,
            pltpu.VMEM((2, order), F32),
            pltpu.VMEM((2, order), F32),
            pltpu.VMEM(row, F32),
            pltpu.VMEM((width + depth, order), F32),
            pltpu.VMEM((width + depth, order), F32),
            pltpu.VMEM((streams * width, order), F32),
            pltpu.VMEM((streams * width, order), F32),
            pltpu.VMEM((streams * width, order), BF16),
            pltpu.VMEM((streams * width, order), BF16),
            *[pltpu.VMEM((width, order), BF16) for _ in range(4)],
            pltpu.VMEM(row, F32),
            *[pltpu.VMEM((chips, *piece), F32) for _ in range(3)],
            pltpu.VMEM((streams, chips, *piece), F32),
            pltpu.VMEM((chips, 1, rows), F32),
            pltpu.VMEM((parts, 1, rows), F32),
            pltpu.VMEM(piece, F32),
            pltpu.VMEM((streams, *piece), F32),
            *[pltpu.VMEM(row, F32) for _ in range(4)],
            dma((parts,)), dma((parts,)), dma((parts,)), dma((parts,)), dma, dma,
            dma((turns + 1,)), dma((turns + 1,)),
            dma((streams * turns,)), dma((streams * turns,)),
            dma((2, streams * turns)), dma((2, streams)),
            dma((streams, chips)), dma((chips,)), dma((span, chips)), dma((chips,)),
            dma((span,)), dma, dma((span, chips)), dma((streams, chips)), dma, dma,
            dma((parts,)), dma((chips,)),
        ],
        compiler_params=pltpu.CompilerParams(
            collective_id=0, has_side_effects=True, vmem_limit_bytes=VMEM_LIMIT
        ),
    )(basis_flux, owner_cell, clogged, conductance, live_count, coupling, leakage, source)


def solution(mesh):
    placed = (
        P("flow", "trans", None),
        P("flow", "trans"),
        P("flow", "trans"),
        P("flow", "trans"),
        P("flow", "trans"),
        P("flow", None),
        P("flow", None),
        P("flow", None),
    )
    return jax.shard_map(
        per_device, mesh=mesh, in_specs=placed, out_specs=P("flow", "trans"), check_vma=False
    )
```

time: 158 us -> 151 us (0.956)
  Pallas kernels: 156 us -> 149 us
    pallas_call x1, Pallas kernels: 156 us -> 149 us  [per_device(): pl.pallas_call(functools.partial(kernel, planes, span, chips, rows, order...]
where the time goes in v4:
time: 151 us
  Pallas kernels  149 us (99%)
    pallas_call x1, Pallas kernels, per_device(): pl.pallas_call(functools.partial(kernel, planes, span, chips, rows, order...  149 us

profile of v4, /device:TPU:1, one launch (start us, length us, event | category | flops | bytes accessed | tf_op | source)
XLA Modules:
  0.0 151.0 jit_solution(243097562093308371)
XLA Ops:
  0.7 149.2 %shard_map.82 = f32[1,128]{1,0:T(1,128)} custom-call(bf16[1,128,1024]{2,1,0:T(8,128)(2,1)} %basis.1, s32[1,128]{1,0:T(1,128)} %owner.1, s32[1,128]{1,0:T(1,128)} %clogged.1, f32[1,128]{1,0:T(1,128)} %conductance.1, s32[1,1]{1,0:T(1,128)S(6)} %copy.10.live, f32[1,1024]{1,0:T(1,128)} %coupling.1, f32[1,1024]{1,0:T(1,128)} %leakage.1, f32[1,1024]{1,0:T(1,128)} %source.1), custom_call_target="tpu_custom_call" | custom-call | tf_op jit(solution)/shard_map/pallas_call | solution.py:624
  149.8 1.2 copy.11

commit v5 on v4

v5 whole, which is shorter than its diff:
```python
import functools

import jax
import jax.numpy as jnp
from jax import lax
from jax.experimental import pallas as pl
from jax.experimental.pallas import tpu as pltpu
from jax.sharding import PartitionSpec as P

MESH = pl.DeviceIdType.MESH
BF16 = jnp.bfloat16
F32 = jnp.float32
VMEM_LIMIT = 56 * 1024 * 1024


def dot(left, right):
    return jnp.dot(left, right, preferred_element_type=F32)


def split(value):
    high = value.astype(BF16)
    return high, (value - high.astype(F32)).astype(BF16)


def kernel(
    planes, span, chips, rows, order, depth, tops,
    basis, owner, clogged, conductance, live, coupling, leakage, source,
    pressure,
    near_high, near_low, inverse_diag,
    slabs, packs, picked, block, gain_high, gain_low, square, faces, faces_in, flux_diag,
    panel_in, panel_out, back_in, back_out, back_high, back_low,
    panel_high, panel_low, last_high, last_low,
    level, parts_out, up_pieces, down_pieces, edge_pieces, end_pieces, end_out,
    edge_up, edges, total, swept_in, swept, system_diag,
    slab_send, slab_recv, pack_send, pack_recv, face_send, face_recv,
    panel_send, panel_recv, back_send, back_recv, held_send, held_recv,
    up_send, up_recv, down_send, down_recv,
    edge_send, edge_recv, mid_send, mid_recv, sweep_send, sweep_recv, end_send, end_recv,
):
    plane = lax.axis_index("flow")
    me = lax.axis_index("trans")
    parts = 2 * chips
    chip, core = me // 2, lax.rem(me, 2)
    partner = me + 1 - 2 * core
    spans = planes // span
    row, spot = plane // span, lax.rem(plane, span)
    row_start = row * span
    last = span - 1
    width = order // chips
    turns = width // depth
    bottoms = tuple(top + 1 for top in tops[1:]) + (0,)
    up_first = jnp.where(row > 0, 0, turns)
    pass_first = jnp.where(jnp.logical_and(row > 0, spot > 0), 0, turns)

    def one_of(places):
        return functools.reduce(jnp.logical_or, [spot == place for place in places])

    first_column = pl.multiple_of(chip * width, width)
    face = coupling[...]
    other_chips = [lax.rem(chip + turn, chips) for turn in range(1, chips)]
    step_rows = 256
    steps = order // step_rows

    barrier = pltpu.get_barrier_semaphore()

    def greet(target_plane, target):
        pl.semaphore_signal(barrier, inc=1, device_id=(target_plane, target), device_id_type=MESH)

    for turn in range(1, parts):
        greet(plane, lax.rem(me + turn, parts))

    @pl.when(plane > 0)
    def _():
        greet(plane - 1, me)

    @pl.when(plane < planes - 1)
    def _():
        greet(plane + 1, me)

    @pl.when(jnp.logical_and(core == 1, jnp.logical_and(row > 0, one_of(tops))))
    def _():
        for other in range(chips):
            greet(row_start - 1, other * 2 + 1)

    def slab(index):
        return slabs.at[:, pl.ds(pl.multiple_of(index * rows, rows), rows)]

    position = lax.broadcasted_iota(jnp.int32, (1, rows), 1)
    weight = (
        conductance[...]
        * (1 - clogged[...]).astype(F32)
        * (position < live[...]).astype(F32)
    ).astype(BF16).astype(F32)
    row_id = lax.broadcasted_iota(jnp.int32, (8, rows), 0)
    packs[me] = jnp.where(row_id == 0, weight, owner[...].astype(F32))
    slabs[:, pl.ds(pl.multiple_of(me * rows, rows), rows)] = basis[0].astype(F32).T.astype(BF16)

    next_to = jnp.where(plane > 0, 1, 0) + jnp.where(plane < planes - 1, 1, 0)
    sends_up = jnp.logical_and(core == 1, jnp.logical_and(spot == last, row < spans - 1))
    extra = jnp.where(sends_up, chips * len(tops), 0)
    pl.semaphore_wait(barrier, parts - 1 + next_to + extra)

    def slab_copy(index, target, slot):
        return pltpu.make_async_remote_copy(
            slab(index), slab(index), slab_send.at[slot], slab_recv.at[index],
            device_id=(plane, target), device_id_type=MESH,
        )

    def pack_copy(index, target, slot):
        return pltpu.make_async_remote_copy(
            packs.at[index], packs.at[index], pack_send.at[slot], pack_recv.at[index],
            device_id=(plane, target), device_id_type=MESH,
        )

    others = [lax.rem(me + turn, parts) for turn in range(1, parts)]
    for slot, target in enumerate(others):
        pack_copy(me, target, slot).start()
    way = 1 - 2 * core
    ahead = lax.rem(chip + way + chips, chips) * 2 + core
    behind = lax.rem(chip - way + chips, chips) * 2 + core
    across_ring = lax.rem(chip + 2, chips) * 2 + core
    slab_copy(me, ahead, 0).start()
    slab_copy(me, behind, 1).start()
    slab_copy(me, partner, 2).start()

    column = lax.broadcasted_iota(jnp.int32, (rows, order), 1).astype(F32)

    def pick(index, carry):
        turned = packs[index].T
        picked[pl.ds(pl.multiple_of(index * rows, rows), rows), :] = jnp.where(
            turned[:, 1:2] == column, turned[:, 0:1], 0.0
        ).astype(BF16)
        return carry

    for other in others:
        pack_copy(other, partner, 0).wait_recv()
    lax.fori_loop(0, parts, pick, 0)

    slab_copy(behind, partner, 0).wait_recv()
    slab_copy(behind, ahead, 3).start()
    slab_copy(behind, partner, 4).start()
    slab_copy(ahead, partner, 0).wait_recv()
    slab_copy(ahead, partner, 5).start()
    slab_copy(across_ring, partner, 0).wait_recv()
    slab_copy(across_ring, partner, 6).start()
    slab_copy(partner, partner, 0).wait_recv()
    flip = 1 - 2 * core
    for source_slab in (behind, ahead, across_ring):
        slab_copy(source_slab + flip, partner, 0).wait_recv()

    eye = lax.broadcasted_iota(jnp.int32, (rows, rows), 0) == lax.broadcasted_iota(
        jnp.int32, (rows, rows), 1
    )
    for index in range(order // rows):
        here = pl.ds(index * rows, rows)
        flux_diag[:, here] = jnp.sum(
            jnp.where(eye, dot(slabs[here, :], picked[:, here]), 0.0), axis=0, keepdims=True
        )

    leak = leakage[...]
    schur = face * face / (face + leak + flux_diag[...])
    faces[0:1, :] = face
    faces[1:2, :] = schur

    def face_copy(target):
        return pltpu.make_async_remote_copy(
            faces, faces_in, face_send, face_recv, device_id=(target, me), device_id_type=MESH
        )

    @pl.when(plane < planes - 1)
    def _():
        face_copy(plane + 1).start()

    def assemble(index, carry):
        here = pl.ds(pl.multiple_of(index * step_rows, step_rows), step_rows)
        block[here, :] = dot(slabs[here, :], picked[...])
        return carry

    lax.fori_loop(0, steps, assemble, 0)

    @pl.when(plane > 0)
    def _():
        face_copy(plane).wait_recv()

    @pl.when(plane == 0)
    def _():
        faces_in[...] = jnp.zeros_like(faces_in)

    diag = flux_diag[...] + (leak + face + faces_in[0:1, :] - faces_in[1:2, :])
    pivots = 1.0 / diag
    inverse_diag[...] = pivots
    system_diag[...] = diag

    across = lax.broadcasted_iota(jnp.int32, (step_rows, order), 1)
    down = lax.broadcasted_iota(jnp.int32, (step_rows, order), 0)

    def scale(index, carry):
        here = pl.ds(pl.multiple_of(index * step_rows, step_rows), step_rows)
        gain = jnp.where(across == down + index * step_rows, 0.0, block[here, :] * pivots)
        block[here, :] = gain
        gain_high[here, :], gain_low[here, :] = split(gain)
        return carry

    lax.fori_loop(0, steps, scale, 0)

    def squared(index, carry):
        here = pl.ds(pl.multiple_of(index * step_rows, step_rows), step_rows)
        high, low = gain_high[here, :], gain_low[here, :]
        value = dot(high, gain_high[...]) + (dot(high, gain_low[...]) + dot(low, gain_high[...]))
        square[here, :] = value.astype(BF16)
        block[here, :] = value - block[here, :]
        return carry

    lax.fori_loop(0, steps, squared, 0)

    def finish(turn, carry):
        index = lax.rem(chip + turn, steps)
        here = pl.ds(pl.multiple_of(index * step_rows, step_rows), step_rows)
        near = block[here, :] - dot(gain_high[here, :], square[...])
        near_high[here, :], near_low[here, :] = split(near)
        return carry

    def remote(source_ref, target_ref, send, recv, target_plane, target):
        return pltpu.make_async_remote_copy(
            source_ref, target_ref, send, recv,
            device_id=(target_plane, target), device_id_type=MESH,
        )

    def apply(value):
        count = value.shape[0]
        scaled = value * inverse_diag[...]
        high = scaled.astype(BF16).astype(F32)
        both = jnp.concatenate([high, scaled - high], axis=0).astype(BF16)
        by_high = dot(both, near_high[...])
        by_low = dot(both[:count], near_low[...])
        return scaled + (by_high[:count] + (by_high[count:] + by_low)), both[:count], both[count:]

    def two_rows(value):
        row_id = lax.broadcasted_iota(jnp.int32, (8, value.shape[1]), 0)
        high = value.astype(BF16).astype(F32)
        return jnp.where(row_id == 0, high, jnp.where(row_id == 1, value - high, 0.0)).astype(BF16)

    def apply_one(value):
        scaled = value * inverse_diag[...]
        both = two_rows(scaled)
        return scaled + jnp.sum(
            dot(both, near_high[...]) + dot(both, near_low[...]), axis=0, keepdims=True
        )

    def by_panel(value, high, low):
        both = two_rows(value)
        return jnp.sum(dot(both, high[...]) + dot(both, low[...]), axis=0, keepdims=True)

    def take(index):
        return pl.ds(pl.multiple_of(index * depth, depth), depth)

    one_hot_row = lax.broadcasted_iota(jnp.int32, (depth, order), 0)
    one_hot_column = lax.broadcasted_iota(jnp.int32, (depth, order), 1)

    def unit_rows(index):
        return jnp.where(
            one_hot_column == one_hot_row + (chip * width + index * depth), 1.0, 0.0
        )

    def back_copy(index):
        return remote(
            back_out.at[take(index), :], back_in.at[take(index), :],
            back_send.at[index], back_recv.at[index], plane - 1, me,
        )

    def held_copy(index, half):
        ref = back_low if half else back_high
        return remote(
            ref.at[take(index), :], ref.at[take(index), :],
            held_send.at[half, index], held_recv.at[half, index // turns], plane, partner,
        )

    def stream_turns(stream):
        active = spot <= tops[stream]
        if stream == 0:
            active = jnp.logical_and(active, row < spans - 1)
        return jnp.where(active, turns, 0)

    def end_copy(target):
        return remote(
            end_out.at[target], end_pieces.at[chip], end_send.at[target], end_recv.at[chip],
            plane, target,
        )

    def end_from(source_chip):
        return remote(
            end_out.at[0], end_pieces.at[source_chip], end_send.at[0], end_recv.at[source_chip],
            plane, me,
        )

    def panel_copy(index):
        return remote(
            panel_out.at[take(index), :], panel_in.at[take(index), :],
            panel_send.at[index], panel_recv.at[index], plane + 1, me,
        )

    finish(0, 0)

    @pl.when(jnp.logical_and(core == 1, jnp.logical_and(spot == 0, row > 0)))
    def _():
        def first(turn, carry):
            here = pl.ds(pl.multiple_of(first_column + turn * depth, depth), depth)
            unit = unit_rows(turn) * pivots
            near = near_high[here, :].astype(F32) + near_low[here, :].astype(F32)
            panel_out[take(turn), :] = face * (unit + jnp.sum(unit, axis=1, keepdims=True) * near)
            panel_copy(turn).start()
            panel_high[take(turn), :], panel_low[take(turn), :] = split(unit)
            return carry

        lax.fori_loop(0, turns, first, 0)

    lax.fori_loop(1, steps, finish, 0)

    @pl.when(core == 0)
    def _():
        def flow_down(stream, top):
            def flow(turn, carry):
                index = stream * turns + turn

                @pl.when(spot == top)
                def _():
                    back_in[take(index), :] = unit_rows(turn)

                @pl.when(spot < top)
                def _():
                    back_copy(index).wait_recv()

                moved = apply(face * back_in[take(index), :])[0]
                back_out[take(index), :] = moved

                @pl.when(spot > 0)
                def _():
                    back_copy(index).start()

                back_high[take(index), :], back_low[take(index), :] = split(moved)
                held_copy(index, 0).start()
                held_copy(index, 1).start()
                return carry

            return flow

        def drain(stream):
            def wait(turn, carry):
                index = stream * turns + turn

                @pl.when(spot > 0)
                def _():
                    back_copy(index).wait_send()

                held_copy(index, 0).wait_send()
                held_copy(index, 1).wait_send()
                return carry

            return wait

        for stream in range(len(tops) - 1, -1, -1):
            lax.fori_loop(0, stream_turns(stream), flow_down(stream, tops[stream]), 0)
        for stream in range(len(tops) - 1, -1, -1):
            lax.fori_loop(0, stream_turns(stream), drain(stream), 0)
        for target in range(chips):
            end_from(target).wait_recv()
        pressure[...] = (end_pieces[0] + end_pieces[1]) + (end_pieces[2] + end_pieces[3])

    def up_copy(target, part):
        return remote(
            parts_out.at[target], up_pieces.at[chip],
            up_send.at[part, target], up_recv.at[chip],
            row_start + span + tops[part], target * 2 + 1,
        )

    def down_copy(target, place):
        return remote(
            parts_out.at[target], down_pieces.at[chip],
            down_send.at[place, target], down_recv.at[chip],
            row_start - span + place, target * 2 + 1,
        )

    def edge_copy(place):
        return remote(
            edge_up, edge_up, edge_send.at[place], edge_recv, row_start + place, me
        )

    def mid_copy(stream, target, place):
        return remote(
            parts_out.at[target], edge_pieces.at[stream, chip],
            mid_send.at[place, target], mid_recv.at[stream, chip],
            row_start + place, target * 2 + 1,
        )

    sweep_copy = remote(swept, swept_in, sweep_send, sweep_recv, plane - 1, me)

    def cut(value, ref, count, size):
        for index in range(count):
            ref[index] = value[:, index * size : (index + 1) * size]

    @pl.when(core == 1)
    def _():
        def flow(index, carry):
            @pl.when(spot > 0)
            def _():
                panel_copy(index).wait_recv()

            @pl.when(index == turns)
            def _():
                @pl.when(spot == 0)
                def _():
                    panel_in[take(index), :] = jnp.zeros((depth, order), F32)

                panel_in[take(index), :] = panel_in[take(index), :] + jnp.where(
                    one_hot_row == 0, source[...], 0.0
                )

            arrived_rows = panel_in[take(index), :]
            scaled = arrived_rows * inverse_diag[...]
            high = scaled.astype(BF16)
            low = (scaled - high.astype(F32)).astype(BF16)
            both = jnp.concatenate([high, low], axis=0)
            def advance(pass_on):
                size = order // 2
                for block in range(order // size):
                    across = slice(block * size, (block + 1) * size)
                    by_high = dot(both, near_high[:, across])
                    by_low = dot(high, near_low[:, across])
                    panel_out[take(index), across] = face[:, across] * (
                        scaled[:, across] + (by_high[:depth] + (by_high[depth:] + by_low))
                    )
                    if pass_on:
                        remote(
                            panel_out.at[take(index), across], panel_in.at[take(index), across],
                            panel_send.at[index], panel_recv.at[index], plane + 1, me,
                        ).start()

            @pl.when(spot < last)
            def _():
                advance(True)

            @pl.when(spot == last)
            def _():
                advance(False)

            @pl.when(index < turns)
            def _():
                panel_high[take(index), :] = high
                panel_low[take(index), :] = low

                @pl.when(spot == last)
                def _():
                    last_high[take(index), :], last_low[take(index), :] = split(
                        panel_out[take(index), :]
                    )

            return carry

        lax.fori_loop(pass_first, turns + 1, flow, 0)
        level[...] = jnp.where(chip == 0, panel_in[width : width + 1, :], 0.0)

        def gather_pieces(pieces, sems):
            for target in range(chips):
                remote(
                    parts_out.at[target], pieces.at[target], end_send.at[0], sems.at[target],
                    plane, me,
                ).wait_recv()
            return (pieces[0] + pieces[1]) + (pieces[2] + pieces[3])

        @pl.when(jnp.logical_and(row > 0, one_of(tops)))
        def _():
            edge_up[...] = gather_pieces(up_pieces, up_recv)

        @pl.when(jnp.logical_and(spot == last, row < spans - 1))
        def _():
            @pl.when(row == 0)
            def _():
                parts_out[...] = jnp.zeros_like(parts_out)

            @pl.when(row > 0)
            def _():
                cut(by_panel(edge_up[...], last_high, last_low), parts_out, chips, width)

            parts_out[chip] = parts_out[chip] + panel_out[
                width : width + 1, pl.ds(first_column, width)
            ]
            for part in range(len(tops)):
                for target in range(chips):
                    up_copy(target, part).start()

        @pl.when(row > 0)
        def _():
            for top, bottom in zip(tops, bottoms):
                @pl.when(spot == top)
                def _():
                    for place in range(top - 1, bottom - 1, -1):
                        edge_copy(place).start()

            @pl.when(jnp.logical_not(one_of(tops)))
            def _():
                edge_copy(0).wait_recv()

            level[...] = level[...] + system_diag[...] * by_panel(
                edge_up[...], panel_high, panel_low
            )

        @pl.when(jnp.logical_not(one_of(tops)))
        def _():
            sweep_copy.wait_recv()
            level[...] = level[...] + face * swept_in[...]

        swept[...] = apply_one(level[...])

        @pl.when(jnp.logical_not(one_of(bottoms)))
        def _():
            sweep_copy.start()

        for stream in range(1, len(tops)):
            @pl.when(spot == bottoms[stream - 1])
            def _():
                cut(swept[...], parts_out, chips, width)

                def send_mid(place, carry):
                    for target in range(chips):
                        mid_copy(stream, target, place).start()
                    return carry

                lax.fori_loop(0, tops[stream] + 1, send_mid, 0)

        def arrived(stream):
            here = pl.ds(stream * width, width)
            for half, ref in enumerate((back_high, back_low)):
                remote(
                    ref.at[here, :], ref.at[here, :],
                    held_send.at[half, 0], held_recv.at[half, stream], plane, me,
                ).wait_recv()

        def by_stream(stream):
            here = slice(stream * width, (stream + 1) * width)
            return by_panel(edges[stream], back_high.at[here, :], back_low.at[here, :])

        total[...] = swept[...]
        for stream in range(len(tops) - 1, -1, -1):
            @pl.when(stream_turns(stream) > 0)
            def _():
                arrived(stream)

        for stream in range(1, len(tops)):
            @pl.when(spot <= tops[stream])
            def _():
                edges[stream] = gather_pieces(edge_pieces.at[stream], mid_recv.at[stream])
                total[...] = total[...] + by_stream(stream)

        @pl.when(row < spans - 1)
        def _():
            edges[0] = gather_pieces(down_pieces, down_recv)
            total[...] = total[...] + by_stream(0)

        @pl.when(jnp.logical_and(spot == 0, row > 0))
        def _():
            cut(total[...], parts_out, chips, width)

            def send_down(place, carry):
                for target in range(chips):
                    down_copy(target, place).start()
                return carry

            lax.fori_loop(0, span, send_down, 0)

        cut(total[...], end_out, parts, rows)
        for target in others:
            end_copy(target).start()
        end_pieces[chip] = end_out[me]
        for other in other_chips:
            end_from(other).wait_recv()
        pressure[...] = (end_pieces[0] + end_pieces[1]) + (end_pieces[2] + end_pieces[3])

        @pl.when(spot < last)
        def _():
            def drain(index, carry):
                panel_copy(index).wait_send()
                return carry

            lax.fori_loop(up_first, turns + 1, drain, 0)

        @pl.when(jnp.logical_and(spot == last, row < spans - 1))
        def _():
            for part in range(len(tops)):
                for target in range(chips):
                    up_copy(target, part).wait_send()

        @pl.when(row > 0)
        def _():
            for top, bottom in zip(tops, bottoms):
                @pl.when(spot == top)
                def _():
                    for place in range(top - 1, bottom - 1, -1):
                        edge_copy(place).wait_send()

        @pl.when(jnp.logical_and(spot == 0, row > 0))
        def _():
            def sent_down(place, carry):
                for target in range(chips):
                    down_copy(target, place).wait_send()
                return carry

            lax.fori_loop(0, span, sent_down, 0)

        for stream in range(1, len(tops)):
            @pl.when(spot == bottoms[stream - 1])
            def _():
                def sent_mid(place, carry):
                    for target in range(chips):
                        mid_copy(stream, target, place).wait_send()
                    return carry

                lax.fori_loop(0, tops[stream] + 1, sent_mid, 0)

        @pl.when(jnp.logical_not(one_of(bottoms)))
        def _():
            sweep_copy.wait_send()

        for target in others:
            end_copy(target).wait_send()

    for slot, target in enumerate(others):
        pack_copy(me, target, slot).wait_send()
    slab_copy(me, ahead, 0).wait_send()
    slab_copy(me, behind, 1).wait_send()
    slab_copy(me, partner, 2).wait_send()
    slab_copy(behind, ahead, 3).wait_send()
    slab_copy(behind, partner, 4).wait_send()
    slab_copy(ahead, partner, 5).wait_send()
    slab_copy(across_ring, partner, 6).wait_send()

    @pl.when(plane < planes - 1)
    def _():
        face_copy(plane + 1).wait_send()


def per_device(basis_flux, owner_cell, clogged, conductance, live_count, coupling, leakage, source):
    planes = lax.axis_size("flow")
    parts = lax.axis_size("trans")
    chips = parts // 2
    rows, order = basis_flux.shape[1:]
    span, depth = planes // 4, 16
    tops = (15, 10, 7, 4)
    streams = len(tops)
    width = order // chips
    turns = width // depth
    row = (1, order)
    piece = (1, width)
    vmem = pl.BlockSpec(memory_space=pltpu.VMEM)
    dma = pltpu.SemaphoreType.DMA
    half = pltpu.VMEM((order, order), BF16)
    return pl.pallas_call(
        functools.partial(kernel, planes, span, chips, rows, order, depth, tops),
        out_shape=jax.ShapeDtypeStruct((1, rows), F32),
        in_specs=[vmem] * 8,
        out_specs=vmem,
        scratch_shapes=[
            half, half, pltpu.VMEM(row, F32),
            half,
            pltpu.VMEM((parts, 8, rows), F32),
            half,
            pltpu.VMEM((order, order), F32),
            half, half, half,
            pltpu.VMEM((2, order), F32),
            pltpu.VMEM((2, order), F32),
            pltpu.VMEM(row, F32),
            pltpu.VMEM((width + depth, order), F32),
            pltpu.VMEM((width + depth, order), F32),
            pltpu.VMEM((streams * width, order), F32),
            pltpu.VMEM((streams * width, order), F32),
            pltpu.VMEM((streams * width, order), BF16),
            pltpu.VMEM((streams * width, order), BF16),
            *[pltpu.VMEM((width, order), BF16) for _ in range(4)],
            pltpu.VMEM(row, F32),
            *[pltpu.VMEM((chips, *piece), F32) for _ in range(3)],
            pltpu.VMEM((streams, chips, *piece), F32),
            pltpu.VMEM((chips, 1, rows), F32),
            pltpu.VMEM((parts, 1, rows), F32),
            pltpu.VMEM(piece, F32),
            pltpu.VMEM((streams, *piece), F32),
            *[pltpu.VMEM(row, F32) for _ in range(4)],
            dma((parts,)), dma((parts,)), dma((parts,)), dma((parts,)), dma, dma,
            dma((turns + 1,)), dma((turns + 1,)),
            dma((streams * turns,)), dma((streams * turns,)),
            dma((2, streams * turns)), dma((2, streams)),
            dma((streams, chips)), dma((chips,)), dma((span, chips)), dma((chips,)),
            dma((span,)), dma, dma((span, chips)), dma((streams, chips)), dma, dma,
            dma((parts,)), dma((chips,)),
        ],
        compiler_params=pltpu.CompilerParams(
            collective_id=0, has_side_effects=True, vmem_limit_bytes=VMEM_LIMIT
        ),
    )(basis_flux, owner_cell, clogged, conductance, live_count, coupling, leakage, source)


def solution(mesh):
    placed = (
        P("flow", "trans", None),
        P("flow", "trans"),
        P("flow", "trans"),
        P("flow", "trans"),
        P("flow", "trans"),
        P("flow", None),
        P("flow", None),
        P("flow", None),
    )
    return jax.shard_map(
        per_device, mesh=mesh, in_specs=placed, out_specs=P("flow", "trans"), check_vma=False
    )
```

time: 151 us -> 147 us (0.974)
  Pallas kernels: 149 us -> 145 us
    pallas_call x1, Pallas kernels: 149 us -> 145 us  [per_device(): pl.pallas_call(functools.partial(kernel, planes, span, chips, rows, order...]
where the time goes in v5:
time: 147 us
  Pallas kernels  145 us (99%)
    pallas_call x1, Pallas kernels, per_device(): pl.pallas_call(functools.partial(kernel, planes, span, chips, rows, order...  145 us

profile of v5, /device:TPU:1, one launch (start us, length us, event | category | flops | bytes accessed | tf_op | source)
XLA Modules:
  0.0 147.2 jit_solution(14562905952108708252)
XLA Ops:
  0.7 145.3 %shard_map.82 = f32[1,128]{1,0:T(1,128)} custom-call(bf16[1,128,1024]{2,1,0:T(8,128)(2,1)} %basis.1, s32[1,128]{1,0:T(1,128)} %owner.1, s32[1,128]{1,0:T(1,128)} %clogged.1, f32[1,128]{1,0:T(1,128)} %conductance.1, s32[1,1]{1,0:T(1,128)S(6)} %copy.10.live, f32[1,1024]{1,0:T(1,128)} %coupling.1, f32[1,1024]{1,0:T(1,128)} %leakage.1, f32[1,1024]{1,0:T(1,128)} %source.1), custom_call_target="tpu_custom_call" | custom-call | tf_op jit(solution)/shard_map/pallas_call | solution.py:656
  146.0 1.2 copy.11

commit v6 on v5

--- a/solution.py
+++ b/solution.py
@@ -92,7 +92,16 @@
         * (position < live[...]).astype(F32)
     ).astype(BF16).astype(F32)
     row_id = lax.broadcasted_iota(jnp.int32, (8, rows), 0)
-    packs[me] = jnp.where(row_id == 0, weight, owner[...].astype(F32))
+    pack = jnp.where(row_id == 0, weight, owner[...].astype(F32))
+    packs[me, 0:8, :] = pack
+    turned = pack.T
+    column = lax.broadcasted_iota(jnp.int32, (rows, order), 1).astype(F32)
+    own_share = jnp.sum(
+        jnp.where(turned[:, 1:2] == column, turned[:, 0:1], 0.0) * basis[0].astype(F32),
+        axis=0, keepdims=True,
+    )
+    for index in range(order // rows):
+        packs[me, 8 + index : 9 + index, :] = own_share[:, index * rows : (index + 1) * rows]
     slabs[:, pl.ds(pl.multiple_of(me * rows, rows), rows)] = basis[0].astype(F32).T.astype(BF16)
 
     next_to = jnp.where(plane > 0, 1, 0) + jnp.where(plane < planes - 1, 1, 0)
@@ -123,60 +132,69 @@
     slab_copy(me, behind, 1).start()
     slab_copy(me, partner, 2).start()
 
-    column = lax.broadcasted_iota(jnp.int32, (rows, order), 1).astype(F32)
+    for other in others:
+        pack_copy(other, partner, 0).wait_recv()
+
+    shares = packs[0, 8:16, :]
+    for index in range(1, parts):
+        shares = shares + packs[index, 8:16, :]
+    for index in range(order // rows):
+        flux_diag[:, index * rows : (index + 1) * rows] = shares[index : index + 1, :]
+    leak = leakage[...]
+    schur = face * face / (face + leak + flux_diag[...])
+    faces[0:1, :] = face
+    faces[1:2, :] = schur
+
+    def face_copy(target):
+        return pltpu.make_async_remote_copy(
+            faces, faces_in, face_send, face_recv, device_id=(target, me), device_id_type=MESH
+        )
+
+    @pl.when(plane < planes - 1)
+    def _():
+        face_copy(plane + 1).start()
 
     def pick(index, carry):
-        turned = packs[index].T
+        turned = packs[index, 0:8, :].T
         picked[pl.ds(pl.multiple_of(index * rows, rows), rows), :] = jnp.where(
             turned[:, 1:2] == column, turned[:, 0:1], 0.0
         ).astype(BF16)
         return carry
 
-    for other in others:
-        pack_copy(other, partner, 0).wait_recv()
     lax.fori_loop(0, parts, pick, 0)
 
+    def chunk(index):
+        return pl.ds(pl.multiple_of(index * step_rows, step_rows), step_rows)
+
+    def from_chip(index, source_chip):
+        slab_rows = pl.ds(pl.multiple_of(source_chip * 2 * rows, 2 * rows), 2 * rows)
+        return dot(slabs[chunk(index), slab_rows], picked[slab_rows, :])
+
+    def begin(index, carry):
+        block[chunk(index), :] = from_chip(index, chip)
+        return carry
+
+    def add_chip(source_chip):
+        def add(index, carry):
+            block[chunk(index), :] = block[chunk(index), :] + from_chip(index, source_chip)
+            return carry
+
+        return add
+
+    flip = 1 - 2 * core
+    slab_copy(partner, partner, 0).wait_recv()
+    lax.fori_loop(0, steps, begin, 0)
     slab_copy(behind, partner, 0).wait_recv()
     slab_copy(behind, ahead, 3).start()
     slab_copy(behind, partner, 4).start()
     slab_copy(ahead, partner, 0).wait_recv()
     slab_copy(ahead, partner, 5).start()
+    slab_copy(ahead + flip, partner, 0).wait_recv()
+    lax.fori_loop(0, steps, add_chip(ahead // 2), 0)
     slab_copy(across_ring, partner, 0).wait_recv()
     slab_copy(across_ring, partner, 6).start()
-    slab_copy(partner, partner, 0).wait_recv()
-    flip = 1 - 2 * core
-    for source_slab in (behind, ahead, across_ring):
-        slab_copy(source_slab + flip, partner, 0).wait_recv()
-
-    eye = lax.broadcasted_iota(jnp.int32, (rows, rows), 0) == lax.broadcasted_iota(
-        jnp.int32, (rows, rows), 1
-    )
-    for index in range(order // rows):
-        here = pl.ds(index * rows, rows)
-        flux_diag[:, here] = jnp.sum(
-            jnp.where(eye, dot(slabs[here, :], picked[:, here]), 0.0), axis=0, keepdims=True
-        )
-
-    leak = leakage[...]
-    schur = face * face / (face + leak + flux_diag[...])
-    faces[0:1, :] = face
-    faces[1:2, :] = schur
-
-    def face_copy(target):
-        return pltpu.make_async_remote_copy(
-            faces, faces_in, face_send, face_recv, device_id=(target, me), device_id_type=MESH
-        )
-
-    @pl.when(plane < planes - 1)
-    def _():
-        face_copy(plane + 1).start()
-
-    def assemble(index, carry):
-        here = pl.ds(pl.multiple_of(index * step_rows, step_rows), step_rows)
-        block[here, :] = dot(slabs[here, :], picked[...])
-        return carry
-
-    lax.fori_loop(0, steps, assemble, 0)
+    slab_copy(behind + flip, partner, 0).wait_recv()
+    lax.fori_loop(0, steps, add_chip(behind // 2), 0)
 
     @pl.when(plane > 0)
     def _():
@@ -195,12 +213,14 @@
     down = lax.broadcasted_iota(jnp.int32, (step_rows, order), 0)
 
     def scale(index, carry):
-        here = pl.ds(pl.multiple_of(index * step_rows, step_rows), step_rows)
-        gain = jnp.where(across == down + index * step_rows, 0.0, block[here, :] * pivots)
+        here = chunk(index)
+        whole = block[here, :] + from_chip(index, across_ring // 2)
+        gain = jnp.where(across == down + index * step_rows, 0.0, whole * pivots)
         block[here, :] = gain
         gain_high[here, :], gain_low[here, :] = split(gain)
         return carry
 
+    slab_copy(across_ring + flip, partner, 0).wait_recv()
     lax.fori_loop(0, steps, scale, 0)
 
     def squared(index, carry):
@@ -661,7 +681,7 @@
         scratch_shapes=[
             half, half, pltpu.VMEM(row, F32),
             half,
-            pltpu.VMEM((parts, 8, rows), F32),
+            pltpu.VMEM((parts, 16, rows), F32),
             half,
             pltpu.VMEM((order, order), F32),
             half, half, half,

time: 147 us -> 144 us (0.980)
  Pallas kernels: 145 us -> 142 us
    pallas_call x1, Pallas kernels: 145 us -> 142 us  [per_device(): pl.pallas_call(functools.partial(kernel, planes, span, chips, rows, order...]
where the time goes in v6:
time: 144 us
  Pallas kernels  142 us (99%)
    pallas_call x1, Pallas kernels, per_device(): pl.pallas_call(functools.partial(kernel, planes, span, chips, rows, order...  142 us

profile of v6, /device:TPU:1, one launch (start us, length us, event | category | flops | bytes accessed | tf_op | source)
XLA Modules:
  0.0 144.0 jit_solution(12008630622983983455)
XLA Ops:
  0.7 142.1 %shard_map.82 = f32[1,128]{1,0:T(1,128)} custom-call(bf16[1,128,1024]{2,1,0:T(8,128)(2,1)} %basis.1, s32[1,128]{1,0:T(1,128)} %owner.1, s32[1,128]{1,0:T(1,128)} %clogged.1, f32[1,128]{1,0:T(1,128)} %conductance.1, s32[1,1]{1,0:T(1,128)S(6)} %copy.10.live, f32[1,1024]{1,0:T(1,128)} %coupling.1, f32[1,1024]{1,0:T(1,128)} %leakage.1, f32[1,1024]{1,0:T(1,128)} %source.1), custom_call_target="tpu_custom_call" | custom-call | tf_op jit(solution)/shard_map/pallas_call | solution.py:676
  142.8 1.2 copy.11

commit v7 on v6

--- a/solution.py
+++ b/solution.py
@@ -27,12 +27,12 @@
     basis, owner, clogged, conductance, live, coupling, leakage, source,
     pressure,
     near_high, near_low, inverse_diag,
-    slabs, packs, picked, block, gain_high, gain_low, square, faces, faces_in, flux_diag,
+    slabs, packs, picked, block, gain_high, gain_low, square, square_low, faces, faces_in, flux_diag,
     panel_in, panel_out, back_in, back_out, back_high, back_low,
     panel_high, panel_low, last_high, last_low,
     level, parts_out, up_pieces, down_pieces, edge_pieces, end_pieces, end_out,
     edge_up, edges, total, swept_in, swept, system_diag,
-    slab_send, slab_recv, pack_send, pack_recv, face_send, face_recv,
+    slab_send, slab_recv, pack_send, pack_recv, face_send, face_recv, square_send, square_recv,
     panel_send, panel_recv, back_send, back_recv, held_send, held_recv,
     up_send, up_recv, down_send, down_recv,
     edge_send, edge_recv, mid_send, mid_recv, sweep_send, sweep_recv, end_send, end_recv,
@@ -223,20 +223,57 @@
     slab_copy(across_ring + flip, partner, 0).wait_recv()
     lax.fori_loop(0, steps, scale, 0)
 
-    def squared(index, carry):
-        here = pl.ds(pl.multiple_of(index * step_rows, step_rows), step_rows)
+    square_rows = 256
+    half_rows = order // 2
+    square_turns = half_rows // square_rows
+    own_half = pl.ds(pl.multiple_of(core * half_rows, half_rows), half_rows)
+    other_half = pl.ds(pl.multiple_of((1 - core) * half_rows, half_rows), half_rows)
+
+    def square_copy(part, turn):
+        ref = square_low if part else square
+        here = pl.ds(pl.multiple_of(core * half_rows + turn * square_rows, square_rows), square_rows)
+        return pltpu.make_async_remote_copy(
+            ref.at[here, :], ref.at[here, :], square_send.at[part, turn], square_recv.at[part],
+            device_id=(plane, partner), device_id_type=MESH,
+        )
+
+    def squared(turn, carry):
+        first_row = turn * square_rows
+        here = pl.ds(pl.multiple_of(core * half_rows + first_row, square_rows), square_rows)
+        there = pl.ds(pl.multiple_of((1 - core) * half_rows + first_row, square_rows), square_rows)
         high, low = gain_high[here, :], gain_low[here, :]
         value = dot(high, gain_high[...]) + (dot(high, gain_low[...]) + dot(low, gain_high[...]))
-        square[here, :] = value.astype(BF16)
+        square[here, :], square_low[here, :] = split(value)
+        square_copy(0, turn).start()
+        square_copy(1, turn).start()
         block[here, :] = value - block[here, :]
+        block[there, :] = -block[there, :]
         return carry
 
-    lax.fori_loop(0, steps, squared, 0)
+    lax.fori_loop(0, square_turns, squared, 0)
+
+    def own_cubic(turn, carry):
+        here = chunk(lax.rem(chip + turn, steps))
+        block[here, :] = block[here, :] - dot(gain_high[here, own_half], square[own_half, :])
+        return carry
+
+    lax.fori_loop(0, steps, own_cubic, 0)
+    for part, ref in enumerate((square, square_low)):
+        pltpu.make_async_remote_copy(
+            ref.at[other_half, :], ref.at[other_half, :],
+            square_send.at[part, 0], square_recv.at[part],
+            device_id=(plane, partner), device_id_type=MESH,
+        ).wait_recv()
 
     def finish(turn, carry):
         index = lax.rem(chip + turn, steps)
-        here = pl.ds(pl.multiple_of(index * step_rows, step_rows), step_rows)
-        near = block[here, :] - dot(gain_high[here, :], square[...])
+        here = chunk(index)
+        add = jnp.where(index // (steps // 2) == core, 0.0, 1.0)
+        near = (
+            block[here, :]
+            - dot(gain_high[here, other_half], square[other_half, :])
+            + add * (square[here, :].astype(F32) + square_low[here, :].astype(F32))
+        )
         near_high[here, :], near_low[here, :] = split(near)
         return carry
 
@@ -645,6 +682,9 @@
 
     for slot, target in enumerate(others):
         pack_copy(me, target, slot).wait_send()
+    for turn in range(square_turns):
+        square_copy(0, turn).wait_send()
+        square_copy(1, turn).wait_send()
     slab_copy(me, ahead, 0).wait_send()
     slab_copy(me, behind, 1).wait_send()
     slab_copy(me, partner, 2).wait_send()
@@ -664,7 +704,7 @@
     chips = parts // 2
     rows, order = basis_flux.shape[1:]
     span, depth = planes // 4, 16
-    tops = (15, 10, 7, 4)
+    tops = (15, 11, 8, 6, 4)
     streams = len(tops)
     width = order // chips
     turns = width // depth
@@ -684,7 +724,7 @@
             pltpu.VMEM((parts, 16, rows), F32),
             half,
             pltpu.VMEM((order, order), F32),
-            half, half, half,
+            half, half, half, half,
             pltpu.VMEM((2, order), F32),
             pltpu.VMEM((2, order), F32),
             pltpu.VMEM(row, F32),
@@ -704,6 +744,7 @@
             pltpu.VMEM((streams, *piece), F32),
             *[pltpu.VMEM(row, F32) for _ in range(4)],
             dma((parts,)), dma((parts,)), dma((parts,)), dma((parts,)), dma, dma,
+            dma((2, 4)), dma((2,)),
             dma((turns + 1,)), dma((turns + 1,)),
             dma((streams * turns,)), dma((streams * turns,)),
             dma((2, streams * turns)), dma((2, streams)),

time: 144 us -> 142 us (0.986)
  Pallas kernels: 142 us -> 140 us
    pallas_call x1, Pallas kernels: 142 us -> 140 us  [per_device(): pl.pallas_call(functools.partial(kernel, planes, span, chips, rows, order...]
where the time goes in v7:
time: 142 us
  Pallas kernels  140 us (99%)
    pallas_call x1, Pallas kernels, per_device(): pl.pallas_call(functools.partial(kernel, planes, span, chips, rows, order...  140 us

profile of v7, /device:TPU:1, one launch (start us, length us, event | category | flops | bytes accessed | tf_op | source)
XLA Modules:
  0.0 141.7 jit_solution(16559914778432370902)
XLA Ops:
  0.7 139.8 %shard_map.82 = f32[1,128]{1,0:T(1,128)} custom-call(bf16[1,128,1024]{2,1,0:T(8,128)(2,1)} %basis.1, s32[1,128]{1,0:T(1,128)} %owner.1, s32[1,128]{1,0:T(1,128)} %clogged.1, f32[1,128]{1,0:T(1,128)} %conductance.1, s32[1,1]{1,0:T(1,128)S(6)} %copy.10.live, f32[1,1024]{1,0:T(1,128)} %coupling.1, f32[1,1024]{1,0:T(1,128)} %leakage.1, f32[1,1024]{1,0:T(1,128)} %source.1), custom_call_target="tpu_custom_call" | custom-call | tf_op jit(solution)/shard_map/pallas_call | solution.py:716
  140.5 1.2 copy.11

commit v8 on v7

--- a/solution.py
+++ b/solution.py
@@ -24,8 +24,9 @@
 
 def kernel(
     planes, span, chips, rows, order, depth, tops,
-    basis, owner, clogged, conductance, live, coupling, leakage, source,
+    basis_in, owner_in, clogged_in, conductance_in, live_in, coupling_in, leakage_in, source_in,
     pressure,
+    basis, owner, clogged, conductance, live, coupling, leakage, source, fetched,
     near_high, near_low, inverse_diag,
     slabs, packs, picked, block, gain_high, gain_low, square, square_low, faces, faces_in, flux_diag,
     panel_in, panel_out, back_in, back_out, back_high, back_low,
@@ -56,11 +57,21 @@
         return functools.reduce(jnp.logical_or, [spot == place for place in places])
 
     first_column = pl.multiple_of(chip * width, width)
-    face = coupling[...]
     other_chips = [lax.rem(chip + turn, chips) for turn in range(1, chips)]
     step_rows = 256
     steps = order // step_rows
 
+    given = (
+        basis_in, owner_in, clogged_in, conductance_in, live_in, coupling_in, leakage_in, source_in
+    )
+    held = (basis, owner, clogged, conductance, live, coupling, leakage, source)
+    fetches = [
+        pltpu.make_async_copy(given[index], held[index], fetched.at[index])
+        for index in range(len(given))
+    ]
+    for fetch in fetches:
+        fetch.start()
+
     barrier = pltpu.get_barrier_semaphore()
 
     def greet(target_plane, target):
@@ -85,6 +96,9 @@
     def slab(index):
         return slabs.at[:, pl.ds(pl.multiple_of(index * rows, rows), rows)]
 
+    for fetch in fetches:
+        fetch.wait()
+    face = coupling[...]
     position = lax.broadcasted_iota(jnp.int32, (1, rows), 1)
     weight = (
         conductance[...]
@@ -699,6 +713,9 @@
 
 
 def per_device(basis_flux, owner_cell, clogged, conductance, live_count, coupling, leakage, source):
+    arguments = (
+        basis_flux, owner_cell, clogged, conductance, live_count, coupling, leakage, source
+    )
     planes = lax.axis_size("flow")
     parts = lax.axis_size("trans")
     chips = parts // 2
@@ -716,9 +733,11 @@
     return pl.pallas_call(
         functools.partial(kernel, planes, span, chips, rows, order, depth, tops),
         out_shape=jax.ShapeDtypeStruct((1, rows), F32),
-        in_specs=[vmem] * 8,
+        in_specs=[pl.BlockSpec(memory_space=pl.ANY)] * 8,
         out_specs=vmem,
         scratch_shapes=[
+            *[pltpu.VMEM(array.shape, array.dtype) for array in arguments],
+            dma((len(arguments),)),
             half, half, pltpu.VMEM(row, F32),
             half,
             pltpu.VMEM((parts, 16, rows), F32),
@@ -755,7 +774,7 @@
         compiler_params=pltpu.CompilerParams(
             collective_id=0, has_side_effects=True, vmem_limit_bytes=VMEM_LIMIT
         ),
-    )(basis_flux, owner_cell, clogged, conductance, live_count, coupling, leakage, source)
+    )(*arguments)
 
 
 def solution(mesh):

time: 142 us -> 141 us (level)
  no operation moved by 1% of the time
where the time goes in v8:
time: 141 us
  Pallas kernels  139 us (99%)
    pallas_call x1, Pallas kernels, per_device(): pl.pallas_call(functools.partial(kernel, planes, span, chips, rows, order...  139 us

profile of v8, /device:TPU:1, one launch (start us, length us, event | category | flops | bytes accessed | tf_op | source)
XLA Modules:
  0.0 140.7 jit_solution(15787733027110365772)
XLA Ops:
  0.7 138.9 %shard_map.82 = f32[1,128]{1,0:T(1,128)} custom-call(bf16[1,128,1024]{2,1,0:T(8,128)(2,1)} %basis_in.1, s32[1,128]{1,0:T(1,128)} %owner_in.1, s32[1,128]{1,0:T(1,128)} %clogged_in.1, f32[1,128]{1,0:T(1,128)} %conductance_in.1, s32[1,1]{1,0:T(1,128)S(6)} %copy.10.live_in, f32[1,1024]{1,0:T(1,128)} %coupling_in.1, f32[1,1024]{1,0:T(1,128)} %leakage_in.1, ...), custom_call_target="tpu_custom_call" | custom-call | tf_op jit(solution)/shard_map/pallas_call | solution.py:733
  139.6 1.2 copy.11

commit v9 on v8

--- a/solution.py
+++ b/solution.py
@@ -43,6 +43,7 @@
     parts = 2 * chips
     chip, core = me // 2, lax.rem(me, 2)
     partner = me + 1 - 2 * core
+    before, after = jnp.maximum(plane - 1, 0), jnp.minimum(plane + 1, planes - 1)
     spans = planes // span
     row, spot = plane // span, lax.rem(plane, span)
     row_start = row * span
@@ -336,7 +337,7 @@
     def back_copy(index):
         return remote(
             back_out.at[take(index), :], back_in.at[take(index), :],
-            back_send.at[index], back_recv.at[index], plane - 1, me,
+            back_send.at[index], back_recv.at[index], before, me,
         )
 
     def held_copy(index, half):
@@ -367,7 +368,7 @@
     def panel_copy(index):
         return remote(
             panel_out.at[take(index), :], panel_in.at[take(index), :],
-            panel_send.at[index], panel_recv.at[index], plane + 1, me,
+            panel_send.at[index], panel_recv.at[index], after, me,
         )
 
     finish(0, 0)
@@ -463,7 +464,7 @@
             row_start + place, target * 2 + 1,
         )
 
-    sweep_copy = remote(swept, swept_in, sweep_send, sweep_recv, plane - 1, me)
+    sweep_copy = remote(swept, swept_in, sweep_send, sweep_recv, before, me)
 
     def cut(value, ref, count, size):
         for index in range(count):
@@ -503,7 +504,7 @@
                     if pass_on:
                         remote(
                             panel_out.at[take(index), across], panel_in.at[take(index), across],
-                            panel_send.at[index], panel_recv.at[index], plane + 1, me,
+                            panel_send.at[index], panel_recv.at[index], after, me,
                         ).start()
 
             @pl.when(spot < last)

time: 141 us -> 141 us (level)
  no operation moved by 1% of the time
where the time goes in v9:
time: 141 us
  Pallas kernels  139 us (99%)
    pallas_call x1, Pallas kernels, per_device(): pl.pallas_call(functools.partial(kernel, planes, span, chips, rows, order...  139 us

profile of v9, /device:TPU:1, one launch (start us, length us, event | category | flops | bytes accessed | tf_op | source)
XLA Modules:
  0.0 140.7 jit_solution(5520790173692944158)
XLA Ops:
  0.7 138.9 %shard_map.82 = f32[1,128]{1,0:T(1,128)} custom-call(bf16[1,128,1024]{2,1,0:T(8,128)(2,1)} %basis_in.1, s32[1,128]{1,0:T(1,128)} %owner_in.1, s32[1,128]{1,0:T(1,128)} %clogged_in.1, f32[1,128]{1,0:T(1,128)} %conductance_in.1, s32[1,1]{1,0:T(1,128)S(6)} %copy.10.live_in, f32[1,1024]{1,0:T(1,128)} %coupling_in.1, f32[1,1024]{1,0:T(1,128)} %leakage_in.1, ...), custom_call_target="tpu_custom_call" | custom-call | tf_op jit(solution)/shard_map/pallas_call | solution.py:734
  139.6 1.2 copy.11
